TPU v7x, 128 devices: a whole 4x4x4 slice. The times are simulated.
128 devices in a mesh: dp: 4 (over z_lo, core), cp: 32 (over y, x, z_hi).
Axes of the slice: x: 4, y: 4, z: 4 (z_hi: 2, z_lo: 2; z = z_hi * 2 + z_lo), core: 2. Of those that a mesh axis runs over, the one named last changes fastest.
Arguments:
- queries: bfloat16 [32768, 4096], P(('dp', 'cp')), may hold values from -6 to 6
- key_states: bfloat16 [32768, 512], P(('dp', 'cp')), may hold values from -6 to 6
- value_states: bfloat16 [32768, 512], P(('dp', 'cp')), may hold values from -6 to 6
- grad_out: bfloat16 [32768, 4096], P(('dp', 'cp')), may hold values from -6 to 6
- token_weight: float32 [32768], P(('dp', 'cp')), may hold values from 0.1 to 9
- span_size: int32 [4, 32], P('dp'), may hold values from 1 to 8, as said below
- short_lengths: int32 [4, 32, 8], P('dp'), may hold values from 1 to 128, 256 in all within a row
Outputs:
- attn_out: bfloat16 [32768, 4096], P(('dp', 'cp'))
- dquery: bfloat16 [32768, 4096], P(('dp', 'cp'))
- dkey: bfloat16 [32768, 512], P(('dp', 'cp'))
- dvalue: bfloat16 [32768, 512], P(('dp', 'cp'))
Inputs may be any that keep to these rules, and one draw needn't show every extreme that they name: `span_size`: along cp, each aligned block of 8 devices of a window is cut into aligned runs of 1, 2, 4 or 8 devices; every device of a run of S devices holds S. Every block of window 0 is one run of 8; window 1's first block holds devices with 1.
All inputs are finite; a program needn't handle non-finite values.
Results may differ from a plain program's by a relative error of at most 0.03.
Values may be sent and summed in bfloat16 or wider, within the bound.
A program may use at most 128 MiB of HBM per device.

v0:
```python
import jax
import jax.numpy as jnp
from jax import lax
from jax.sharding import PartitionSpec as P

HEADS = 32
KV_HEADS = 4
HEAD_DIM = 128
SPAN_MAX = 8


NEG = -1e30


def passed_along(value, axis, steps):
    count = lax.axis_size(axis)
    leading, last = (max(0, -steps), min(count, count - steps))
    return lax.ppermute(value, axis, [(source, source + steps) for source in range(leading, last)])


def token_meta(span_row, length_rows, device, row_count, slot_count):
    span_len = lax.dynamic_index_in_dim(span_row, device, 0, keepdims=False)
    doc_lengths = lax.dynamic_index_in_dim(length_rows, device, 0, keepdims=False)
    half_rows = row_count // 2
    member_rank = device % span_len
    row_ids = jnp.arange(row_count, dtype=jnp.int32)
    fold_index = jnp.where(row_ids < half_rows, member_rank, 2 * span_len - 1 - member_rank)
    spread_pos = fold_index * half_rows + row_ids % half_rows
    doc_ends = jnp.cumsum(doc_lengths)
    slot_ids = jnp.sum((row_ids[:, None] >= doc_ends[None, :]).astype(jnp.int32), axis=1)
    doc_starts = doc_ends - doc_lengths
    one_hot = slot_ids[:, None] == jnp.arange(slot_count, dtype=jnp.int32)[None, :]
    local_pos = row_ids - jnp.sum(jnp.where(one_hot, doc_starts[None, :], 0), axis=1)
    spread = span_len > 1
    position = jnp.where(spread, spread_pos, local_pos)
    document = jnp.where(
        spread, (device - member_rank) * slot_count, device * slot_count + slot_ids
    )
    return (position, document)


def on_device(queries, key_states, value_states, grad_out, token_weight, span_size, short_lengths):
    row_count = queries.shape[0]
    kv_width = key_states.shape[1]
    groups = HEADS // KV_HEADS
    span_limit = SPAN_MAX
    half_rows = row_count // 2
    query_rows = row_count // 4
    block_total = 2 * span_limit
    softmax_scale = HEAD_DIM ** (-0.5)
    device = lax.axis_index("cp")
    member_rank = device % span_limit
    block_base = device - member_rank
    span_row = span_size[0]
    length_rows = short_lengths[0]
    slot_count = length_rows.shape[1]
    my_pos, my_doc = token_meta(span_row, length_rows, device, row_count, slot_count)
    members = block_base + jnp.arange(span_limit, dtype=jnp.int32)
    peer_pos, peer_doc = jax.vmap(
        lambda member: token_meta(span_row, length_rows, member, row_count, slot_count)
    )(members)
    weight_sum = lax.psum(jnp.sum(token_weight), ("dp", "cp"))
    mean_weight = weight_sum / (row_count * lax.axis_size("dp") * lax.axis_size("cp"))
    dout = (token_weight[:, None] * grad_out.astype(jnp.float32) / mean_weight).astype(jnp.bfloat16)
    kv_pair = jnp.concatenate([key_states, value_states], axis=1)
    gathered = jnp.zeros((span_limit,) + kv_pair.shape, jnp.bfloat16)
    gathered = lax.dynamic_update_index_in_dim(gathered, kv_pair, member_rank, 0)
    rising = kv_pair
    falling = kv_pair
    for step_index in range(1, span_limit):
        rising = passed_along(rising, "cp", 1)
        falling = passed_along(falling, "cp", -1)
        below_ok = member_rank >= step_index
        gathered = jnp.where(
            below_ok,
            lax.dynamic_update_index_in_dim(
                gathered, rising, (member_rank - step_index) % span_limit, 0
            ),
            gathered,
        )
        above_ok = member_rank + step_index < span_limit
        gathered = jnp.where(
            above_ok,
            lax.dynamic_update_index_in_dim(
                gathered, falling, (member_rank + step_index) % span_limit, 0
            ),
            gathered,
        )
    key_blocks = gathered.reshape(block_total, half_rows, 2 * kv_width)
    key_pos = peer_pos.reshape(block_total, half_rows)
    key_doc = peer_doc.reshape(block_total, half_rows)

    def block_parts(block_index, query_pos, query_doc):
        block_data = lax.dynamic_index_in_dim(key_blocks, block_index, 0, keepdims=False)
        keys_part = block_data[:, :kv_width].reshape(half_rows, KV_HEADS, HEAD_DIM)
        values_part = block_data[:, kv_width:].reshape(half_rows, KV_HEADS, HEAD_DIM)
        block_pos = lax.dynamic_index_in_dim(key_pos, block_index, 0, keepdims=False)
        block_doc = lax.dynamic_index_in_dim(key_doc, block_index, 0, keepdims=False)
        visible = (query_doc[:, None] == block_doc[None, :]) & (
            block_pos[None, :] <= query_pos[:, None]
        )
        return (keys_part, values_part, visible)

    def scores_of(query_part, keys_part):
        return (
            jnp.einsum("qkgd,skd->kgqs", query_part, keys_part, preferred_element_type=jnp.float32)
            * softmax_scale
        )

    def log_totals(query_part, query_pos, query_doc):
        start = (
            jnp.full((KV_HEADS, groups, query_rows), NEG, jnp.float32),
            jnp.zeros((KV_HEADS, groups, query_rows), jnp.float32),
            jnp.full((block_total, KV_HEADS, groups, query_rows, half_rows), NEG, jnp.float32),
        )

        def log_visit_block(block_index, carry):
            keys_part, values_part, visible = block_parts(block_index, query_pos, query_doc)

            def log_attend(state):
                row_max, row_sum, kept = state
                scores = jnp.where(visible, scores_of(query_part, keys_part), NEG)
                new_max = jnp.maximum(row_max, jnp.max(scores, axis=-1))
                fresh = jnp.sum(
                    jnp.where(visible, jnp.exp(scores - new_max[..., None]), 0.0), axis=-1
                )
                kept = lax.dynamic_update_index_in_dim(kept, scores, block_index, 0)
                return (new_max, row_sum * jnp.exp(row_max - new_max) + fresh, kept)

            return lax.cond(jnp.any(visible), log_attend, lambda state: state, carry)

        row_max, row_sum, kept = lax.fori_loop(0, block_total, log_visit_block, start)
        return (row_max + jnp.log(row_sum), kept)

    query_all = queries.reshape(row_count, KV_HEADS, groups, HEAD_DIM)
    dout_all = dout.reshape(row_count, KV_HEADS, groups, HEAD_DIM)
    outputs = []
    dqueries = []
    dkv_total = jnp.zeros((block_total, half_rows, 2 * kv_width), jnp.float32)
    for part_index in range(4):
        first_row = part_index * query_rows
        query_part = query_all[first_row : first_row + query_rows]
        dout_part = dout_all[first_row : first_row + query_rows]
        query_pos = my_pos[first_row : first_row + query_rows]
        query_doc = my_doc[first_row : first_row + query_rows]
        log_total, kept = log_totals(query_part, query_pos, query_doc)

        def attend_visit_block(block_index, running):
            keys_part, values_part, visible = block_parts(block_index, query_pos, query_doc)

            def attend_attend(total):
                scores = lax.dynamic_index_in_dim(kept, block_index, 0, keepdims=False)
                probs = jnp.where(visible, jnp.exp(scores - log_total[..., None]), 0.0)
                return total + jnp.einsum(
                    "kgqs,skd->qkgd",
                    probs.astype(jnp.bfloat16),
                    values_part,
                    preferred_element_type=jnp.float32,
                )

            return lax.cond(jnp.any(visible), attend_attend, lambda total: total, running)

        summed = lax.fori_loop(
            0,
            block_total,
            attend_visit_block,
            jnp.zeros((query_rows, KV_HEADS, groups, HEAD_DIM), jnp.float32),
        )
        out_part = summed.astype(jnp.bfloat16)
        delta = jnp.einsum(
            "qkgd,qkgd->kgq", dout_part, out_part, preferred_element_type=jnp.float32
        )

        def backward_visit_block(block_index, carry):
            keys_part, values_part, visible = block_parts(block_index, query_pos, query_doc)

            def backward_attend(state):
                dquery_sum, dkv_sum = state
                probs = jnp.where(
                    visible, jnp.exp(scores_of(query_part, keys_part) - log_total[..., None]), 0.0
                )
                probs_low = probs.astype(jnp.bfloat16)
                dprobs = jnp.einsum(
                    "qkgd,skd->kgqs", dout_part, values_part, preferred_element_type=jnp.float32
                )
                dscore = (probs * (dprobs - delta[..., None])).astype(jnp.bfloat16)
                dquery_sum = dquery_sum + jnp.einsum(
                    "kgqs,skd->qkgd", dscore, keys_part, preferred_element_type=jnp.float32
                )
                dkeys = jnp.einsum(
                    "kgqs,qkgd->skd", dscore, query_part, preferred_element_type=jnp.float32
                )
                dvalues = jnp.einsum(
                    "kgqs,qkgd->skd", probs_low, dout_part, preferred_element_type=jnp.float32
                )
                update = jnp.concatenate(
                    [dkeys.reshape(half_rows, kv_width), dvalues.reshape(half_rows, kv_width)],
                    axis=1,
                )
                current = lax.dynamic_index_in_dim(dkv_sum, block_index, 0, keepdims=False)
                dkv_sum = lax.dynamic_update_index_in_dim(dkv_sum, current + update, block_index, 0)
                return (dquery_sum, dkv_sum)

            return lax.cond(jnp.any(visible), backward_attend, lambda state: state, carry)

        backward_start = (
            jnp.zeros((query_rows, KV_HEADS, groups, HEAD_DIM), jnp.float32),
            dkv_total,
        )
        dquery_sum, dkv_total = lax.fori_loop(0, block_total, backward_visit_block, backward_start)
        outputs.append(out_part.reshape(query_rows, HEADS * HEAD_DIM))
        dqueries.append(
            (dquery_sum * softmax_scale).astype(jnp.bfloat16).reshape(query_rows, HEADS * HEAD_DIM)
        )
    dkv_shards = dkv_total.reshape(span_limit, row_count, 2 * kv_width)

    def owed_term(target):
        valid = (target >= 0) & (target < span_limit)
        term = lax.dynamic_index_in_dim(dkv_shards, target % span_limit, 0, keepdims=False)
        return jnp.where(valid, term, 0.0)

    upward = owed_term(member_rank - (span_limit - 1))
    downward = owed_term(member_rank + (span_limit - 1))
    for step_index in range(1, span_limit):
        from_above = passed_along(upward.astype(jnp.bfloat16), "cp", -1).astype(upward.dtype)
        from_below = passed_along(downward.astype(jnp.bfloat16), "cp", 1).astype(downward.dtype)
        from_above = jnp.where(member_rank < span_limit - 1, from_above, 0.0)
        from_below = jnp.where(member_rank > 0, from_below, 0.0)
        upward = from_above + owed_term(member_rank - (span_limit - 1) + step_index)
        if step_index < span_limit - 1:
            downward = from_below + owed_term(member_rank + (span_limit - 1) - step_index)
        else:
            downward = from_below
    owned = upward + downward
    dkey = (owned[:, :kv_width] * softmax_scale).astype(jnp.bfloat16)
    dvalue = owned[:, kv_width:].astype(jnp.bfloat16)
    return (jnp.concatenate(outputs, axis=0), jnp.concatenate(dqueries, axis=0), dkey, dvalue)


def solution(mesh):
    in_specs = (
        P(("dp", "cp"), None),
        P(("dp", "cp"), None),
        P(("dp", "cp"), None),
        P(("dp", "cp"), None),
        P(("dp", "cp")),
        P("dp", None),
        P("dp", None, None),
    )
    out_specs = (
        P(("dp", "cp"), None),
        P(("dp", "cp"), None),
        P(("dp", "cp"), None),
        P(("dp", "cp"), None),
    )
    return jax.shard_map(
        on_device, mesh=mesh, in_specs=in_specs, out_specs=out_specs, check_vma=False
    )
```

profile of v0, /device:TPU:8, one launch (start us, length us, event | category | flops | bytes accessed | tf_op | source)
XLA Modules:
  0.0 1275.6 jit_solution(13723392560097350122)
XLA Ops:
  18.2 73.1 %psum.7 = f32[]{:T(128)} all-reduce(f32[]{:T(128)} %reduce_sum.95), channel_id=1, replica_groups=mesh['dp'=4,'cp'=32] {'dp','cp'}, use_global_device_ids=true, to_apply=%region_55.56 | all-reduce | flops 1 | bytes 8 | tf_op jit(solution)/shard_map/psum | solution.py:62
  117.8 13.2 %collective-permute-done.2 = bf16[256,1024]{1,0:T(8,128)(2,1)} collective-permute-done((bf16[256,1024]{1,0:T(8,128)(2,1)}, bf16[256,1024]{1,0:T(8,128)(2,1)}, u32[]{:S(2)}, u32[]{:S(2)}) %collective-permute-start.2) | collective-permute-done | bytes 524320 | tf_op jit(solution)/shard_map/ppermute | solution.py:18
  243.4 11.0 collective-permute-start.13
  278.5 73.6 %while.198 = (s32[]{:T(128)}, f32[4,8,64]{2,1,0:T(8,128)S(1)}, f32[4,8,64]{2,1,0:T(8,128)S(1)}, f32[16,4,8,64,128]{4,3,2,1,0:T(8,128)}, s32[64]{0:T(128)S(1)}, /...) while((s32[]{:T(128)}, f32[4,8,64]{2,1,0:T(8,128)S(1)}, ...), condition=%wide.region_48.49_spmd, body=%wide.region_42.48_spmd.sunk | while | flops 68718592 | bytes 5771033 | solution.py:132
  352.2 68.7 %while.199 = (s32[]{:T(128)}, f32[64,4,8,128]{3,0,2,1:T(8,128)S(1)}, s32[64]{0:T(128)S(1)}, s32[16,128]{1,0:T(8,128)S(1)}, s32[16,128]{1,0:T(8,128)S(1)}, /*inde...) while((s32[]{:T(128)}, f32[64,4,8,128]{3,0,2,1:T(8,128)S(1)}, ...), condition=%wide.region_53.54_spmd, body=%wide.region_49.53_spmd.sunk | while | flops 68190208 | bytes 4091609 | solution.py:163
  428.8 74.9 %while.196 = (s32[]{:T(128)}, f32[4,8,64]{2,1,0:T(8,128)S(1)}, f32[4,8,64]{2,1,0:T(8,128)S(1)}, f32[16,4,8,64,128]{4,3,2,1,0:T(8,128)}, s32[64]{0:T(128)S(1)}, /...) while((s32[]{:T(128)}, f32[4,8,64]{2,1,0:T(8,128)S(1)}, ...), condition=%wide.region_36.37_spmd, body=%wide.region_30.36_spmd.sunk | while | flops 68718592 | bytes 5771033 | solution.py:132
  503.9 68.7 %while.197 = (s32[]{:T(128)}, f32[64,4,8,128]{3,0,2,1:T(8,128)S(1)}, s32[64]{0:T(128)S(1)}, s32[16,128]{1,0:T(8,128)S(1)}, s32[16,128]{1,0:T(8,128)S(1)}, /*inde...) while((s32[]{:T(128)}, f32[64,4,8,128]{3,0,2,1:T(8,128)S(1)}, ...), condition=%wide.region_41.42_spmd, body=%wide.region_37.41_spmd.sunk | while | flops 68190208 | bytes 4091609 | solution.py:163
  580.5 26.1 %while.194 = (s32[]{:T(128)}, f32[4,8,64]{2,1,0:T(8,128)S(1)}, f32[4,8,64]{2,1,0:T(8,128)S(1)}, f32[16,4,8,64,128]{4,3,2,1,0:T(8,128)}, s32[64]{0:T(128)S(1)}, /...) while((s32[]{:T(128)}, f32[4,8,64]{2,1,0:T(8,128)S(1)}, ...), condition=%wide.region_24.25_spmd, body=%wide.region_18.24_spmd.sunk | while | flops 68718592 | bytes 5771033 | solution.py:132
  606.7 25.6 %while.195 = (s32[]{:T(128)}, f32[64,4,8,128]{3,0,2,1:T(8,128)S(1)}, s32[64]{0:T(128)S(1)}, s32[16,128]{1,0:T(8,128)S(1)}, s32[16,128]{1,0:T(8,128)S(1)}, /*inde...) while((s32[]{:T(128)}, f32[64,4,8,128]{3,0,2,1:T(8,128)S(1)}, ...), condition=%wide.region_29.30_spmd, body=%wide.region_25.29_spmd.sunk | while | flops 68190208 | bytes 4091609 | solution.py:163
  640.3 26.2 %while.192 = (s32[]{:T(128)}, f32[4,8,64]{2,1,0:T(8,128)S(1)}, f32[4,8,64]{2,1,0:T(8,128)S(1)}, f32[16,4,8,64,128]{4,3,2,1,0:T(8,128)}, s32[64]{0:T(128)S(1)}, /...) while((s32[]{:T(128)}, f32[4,8,64]{2,1,0:T(8,128)S(1)}, ...), condition=%wide.region_12.13_spmd, body=%wide.region_6.12_spmd.sunk | while | flops 68718592 | bytes 5771033 | solution.py:132
  666.6 25.6 %while.193 = (s32[]{:T(128)}, f32[64,4,8,128]{3,0,2,1:T(8,128)S(1)}, s32[64]{0:T(128)S(1)}, s32[16,128]{1,0:T(8,128)S(1)}, s32[16,128]{1,0:T(8,128)S(1)}, /*inde...) while((s32[]{:T(128)}, f32[64,4,8,128]{3,0,2,1:T(8,128)S(1)}, ...), condition=%wide.region_17.18_spmd, body=%wide.region_13.17_spmd.sunk | while | flops 68190208 | bytes 4091609 | solution.py:163
  700.3 33.7 %while.200 = (s32[]{:T(128)}, f32[64,4,8,128]{3,0,2,1:T(8,128)}, f32[16,128,1024]{1,2,0:T(8,128)}, s32[64]{0:T(128)S(1)}, s32[16,128]{1,0:T(8,128)S(1)}, /*index...) while((s32[]{:T(128)}, f32[64,4,8,128]{3,0,2,1:T(8,128)}, ...), condition=%wide.region_60.61_spmd, body=%wide.region_56.60_spmd.sunk | while | flops 337936384 | bytes 14585669 | solution.py:210
  701.7 10.9 conditional.32
  738.2 31.9 %while.201 = (s32[]{:T(128)}, f32[64,4,8,128]{3,0,2,1:T(8,128)}, f32[16,128,1024]{1,2,0:T(8,128)}, s32[64]{0:T(128)S(1)}, s32[16,128]{1,0:T(8,128)S(1)}, /*index...) while((s32[]{:T(128)}, f32[64,4,8,128]{3,0,2,1:T(8,128)}, ...), condition=%wide.region_65.66_spmd, body=%wide.region_61.65_spmd.sunk | while | flops 337936384 | bytes 12488489 | solution.py:210
  739.6 9.1 conditional.33
  774.3 167.7 %while.202 = (s32[]{:T(128)}, f32[64,4,8,128]{3,0,2,1:T(8,128)}, f32[16,128,1024]{1,2,0:T(8,128)}, s32[64]{0:T(128)S(1)}, s32[16,128]{1,0:T(8,128)S(1)}, /*index...) while((s32[]{:T(128)}, f32[64,4,8,128]{3,0,2,1:T(8,128)}, ...), condition=%wide.region_70.71_spmd, body=%wide.region_66.70_spmd.sunk | while | flops 337936384 | bytes 12488489 | solution.py:210
  775.7 9.1 conditional.34
  786.2 9.1 conditional.34
  807.1 9.1 conditional.34
  817.5 9.1 conditional.34
  838.5 9.1 conditional.34
  848.9 9.1 conditional.34
  859.4 9.1 conditional.34
  869.9 9.1 conditional.34
  890.8 9.1 conditional.34
  901.3 9.1 conditional.34
  911.8 9.1 conditional.34
  922.2 9.1 conditional.34
  932.7 9.1 conditional.34
  945.4 133.1 %while.203 = (s32[]{:T(128)}, f32[64,4,8,128]{3,0,2,1:T(8,128)}, f32[16,128,1024]{1,2,0:T(8,128)}, s32[64]{0:T(128)S(1)}, s32[16,128]{1,0:T(8,128)S(1)}, /*index...) while((s32[]{:T(128)}, f32[64,4,8,128]{3,0,2,1:T(8,128)}, ...), condition=%wide.region_75.76_spmd, body=%wide.region_71.75_spmd.sunk | while | flops 337936384 | bytes 12488489 | solution.py:210
  1078.5 9.3 copy.170
  1089.7 34.3 %collective-permute-start.14 = (bf16[256,1024]{1,0:T(8,128)(2,1)S(1)}, bf16[256,1024]{1,0:T(8,128)(2,1)S(1)}, u32[]{:S(2)}, u32[]{:S(2)}) collective-permute-start(bf16[256,1024]{1,0:T(8,128)(2,1)S(1)} %get-tuple-element.3566), channel_id=1, source_target_pairs={{1,0},{2,1},{3,2},{4,3},{5,4},{6,5},{7,6},{8,7},{9,8},{10,9},{11,1... | collective-permute-start | bytes 1572872 | tf_op jit(solution)/shard_map/ppermute | solution.py:18
  (1436 shorter events, 1344.1 us)
Async XLA Ops:
  0.6 13.8 %copy-start = (s32[1,32]{1,0:T(1,128)S(1)}, s32[1,32]{1,0:T(1,128)}, u32[]{:S(2)}) copy-start(s32[1,32]{1,0:T(1,128)} %param.60) | copy-start | bytes 388
  4.0 101.0 %collective-permute-start = (bf16[256,1024]{1,0:T(8,128)(2,1)}, bf16[256,1024]{1,0:T(8,128)(2,1)}, u32[]{:S(2)}, u32[]{:S(2)}) collective-permute-start(bf16[256,1024]{1,0:T(8,128)(2,1)} %constant_dynamic-update-slice_fusion), channel_id=1, source_target_pairs={{0,1},{1,2},{2,3},{3,4},{4,5},{5,6},{6,7},{7,8},{8,9},{9,10},{10,1... | collective-permute-start | bytes 1572872 | tf_op jit(solution)/shard_map/ppermute | solution.py:18
  9.8 98.7 %collective-permute-start.1 = (bf16[256,1024]{1,0:T(8,128)(2,1)}, bf16[256,1024]{1,0:T(8,128)(2,1)}, u32[]{:S(2)}, u32[]{:S(2)}) collective-permute-start(bf16[256,1024]{1,0:T(8,128)(2,1)} %constant_dynamic-update-slice_fusion), channel_id=1, source_target_pairs={{1,0},{2,1},{3,2},{4,3},{5,4},{6,5},{7,6},{8,7},{9,8},{10,9},{11,1... | collective-permute-start | bytes 1572872 | tf_op jit(solution)/shard_map/ppermute | solution.py:18
  105.0 26.1 %collective-permute-start.2 = (bf16[256,1024]{1,0:T(8,128)(2,1)}, bf16[256,1024]{1,0:T(8,128)(2,1)}, u32[]{:S(2)}, u32[]{:S(2)}) collective-permute-start(bf16[256,1024]{1,0:T(8,128)(2,1)} %collective-permute-done), channel_id=1, source_target_pairs={{0,1},{1,2},{2,3},{3,4},{4,5},{5,6},{6,7},{7,8},{8,9},{9,10},{10,1... | collective-permute-start | bytes 1572872 | tf_op jit(solution)/shard_map/ppermute | solution.py:18
  108.5 32.9 %collective-permute-start.3 = (bf16[256,1024]{1,0:T(8,128)(2,1)}, bf16[256,1024]{1,0:T(8,128)(2,1)}, u32[]{:S(2)}, u32[]{:S(2)}) collective-permute-start(bf16[256,1024]{1,0:T(8,128)(2,1)} %collective-permute-done.1), channel_id=1, source_target_pairs={{1,0},{2,1},{3,2},{4,3},{5,4},{6,5},{7,6},{8,7},{9,8},{10,9},{11,1... | collective-permute-start | bytes 1572872 | tf_op jit(solution)/shard_map/ppermute | solution.py:18
  131.1 27.7 %collective-permute-start.4 = (bf16[256,1024]{1,0:T(8,128)(2,1)}, bf16[256,1024]{1,0:T(8,128)(2,1)}, u32[]{:S(2)}, u32[]{:S(2)}) collective-permute-start(bf16[256,1024]{1,0:T(8,128)(2,1)} %collective-permute-done.2), channel_id=1, source_target_pairs={{0,1},{1,2},{2,3},{3,4},{4,5},{5,6},{6,7},{7,8},{8,9},{9,10},{10,1... | collective-permute-start | bytes 1572872 | tf_op jit(solution)/shard_map/ppermute | solution.py:18
  141.4 25.4 %collective-permute-start.5 = (bf16[256,1024]{1,0:T(8,128)(2,1)}, bf16[256,1024]{1,0:T(8,128)(2,1)}, u32[]{:S(2)}, u32[]{:S(2)}) collective-permute-start(bf16[256,1024]{1,0:T(8,128)(2,1)} %collective-permute-done.3), channel_id=1, source_target_pairs={{1,0},{2,1},{3,2},{4,3},{5,4},{6,5},{7,6},{8,7},{9,8},{10,9},{11,1... | collective-permute-start | bytes 1572872 | tf_op jit(solution)/shard_map/ppermute | solution.py:18
  158.7 26.7 %collective-permute-start.6 = (bf16[256,1024]{1,0:T(8,128)(2,1)}, bf16[256,1024]{1,0:T(8,128)(2,1)S(1)}, u32[]{:S(2)}, u32[]{:S(2)}) collective-permute-start(bf16[256,1024]{1,0:T(8,128)(2,1)} %collective-permute-done.4), channel_id=1, source_target_pairs={{0,1},{1,2},{2,3},{3,4},{4,5},{5,6},{6,7},{7,8},{8,9},{9,10},{10,1... | collective-permute-start | bytes 1572872 | tf_op jit(solution)/shard_map/ppermute | solution.py:18
  166.8 26.6 %collective-permute-start.7 = (bf16[256,1024]{1,0:T(8,128)(2,1)}, bf16[256,1024]{1,0:T(8,128)(2,1)S(1)}, u32[]{:S(2)}, u32[]{:S(2)}) collective-permute-start(bf16[256,1024]{1,0:T(8,128)(2,1)} %collective-permute-done.5), channel_id=1, source_target_pairs={{1,0},{2,1},{3,2},{4,3},{5,4},{6,5},{7,6},{8,7},{9,8},{10,9},{11,1... | collective-permute-start | bytes 1572872 | tf_op jit(solution)/shard_map/ppermute | solution.py:18
  185.5 25.4 %collective-permute-start.8 = (bf16[256,1024]{1,0:T(8,128)(2,1)S(1)}, bf16[256,1024]{1,0:T(8,128)(2,1)S(1)}, u32[]{:S(2)}, u32[]{:S(2)}) collective-permute-start(bf16[256,1024]{1,0:T(8,128)(2,1)S(1)} %collective-permute-done.6), channel_id=1, source_target_pairs={{0,1},{1,2},{2,3},{3,4},{4,5},{5,6},{6,7},{7,8},{8,9},{9,10},{10,1... | collective-permute-start | bytes 1572872 | tf_op jit(solution)/shard_map/ppermute | solution.py:18
  193.5 25.4 %collective-permute-start.9 = (bf16[256,1024]{1,0:T(8,128)(2,1)S(1)}, bf16[256,1024]{1,0:T(8,128)(2,1)S(1)}, u32[]{:S(2)}, u32[]{:S(2)}) collective-permute-start(bf16[256,1024]{1,0:T(8,128)(2,1)S(1)} %collective-permute-done.7), channel_id=1, source_target_pairs={{1,0},{2,1},{3,2},{4,3},{5,4},{6,5},{7,6},{8,7},{9,8},{10,9},{11,1... | collective-permute-start | bytes 1572872 | tf_op jit(solution)/shard_map/ppermute | solution.py:18
  210.9 24.6 %collective-permute-start.10 = (bf16[256,1024]{1,0:T(8,128)(2,1)S(1)}, bf16[256,1024]{1,0:T(8,128)(2,1)S(1)}, u32[]{:S(2)}, u32[]{:S(2)}) collective-permute-start(bf16[256,1024]{1,0:T(8,128)(2,1)S(1)} %collective-permute-done.8), channel_id=1, source_target_pairs={{0,1},{1,2},{2,3},{3,4},{4,5},{5,6},{6,7},{7,8},{8,9},{9,10},{10,1... | collective-permute-start | bytes 1572872 | tf_op jit(solution)/shard_map/ppermute | solution.py:18
  218.8 24.6 %collective-permute-start.11 = (bf16[256,1024]{1,0:T(8,128)(2,1)S(1)}, bf16[256,1024]{1,0:T(8,128)(2,1)S(1)}, u32[]{:S(2)}, u32[]{:S(2)}) collective-permute-start(bf16[256,1024]{1,0:T(8,128)(2,1)S(1)} %collective-permute-done.9), channel_id=1, source_target_pairs={{1,0},{2,1},{3,2},{4,3},{5,4},{6,5},{7,6},{8,7},{9,8},{10,9},{11,1... | collective-permute-start | bytes 1572872 | tf_op jit(solution)/shard_map/ppermute | solution.py:18
  235.5 23.7 %collective-permute-start.12 = (bf16[256,1024]{1,0:T(8,128)(2,1)S(1)}, bf16[256,1024]{1,0:T(8,128)(2,1)S(1)}, u32[]{:S(2)}, u32[]{:S(2)}) collective-permute-start(bf16[256,1024]{1,0:T(8,128)(2,1)S(1)} %collective-permute-done.10), channel_id=1, source_target_pairs={{0,1},{1,2},{2,3},{3,4},{4,5},{5,6},{6,7},{7,8},{8,9},{9,10},{10,1... | collective-permute-start | bytes 1572872 | tf_op jit(solution)/shard_map/ppermute | solution.py:18
  243.4 18.8 %collective-permute-start.13 = (bf16[256,1024]{1,0:T(8,128)(2,1)S(1)}, bf16[256,1024]{1,0:T(8,128)(2,1)S(1)}, u32[]{:S(2)}, u32[]{:S(2)}) collective-permute-start(bf16[256,1024]{1,0:T(8,128)(2,1)S(1)} %collective-permute-done.11), channel_id=1, source_target_pairs={{1,0},{2,1},{3,2},{4,3},{5,4},{6,5},{7,6},{8,7},{9,8},{10,9},{11,1... | collective-permute-start | bytes 1572872 | tf_op jit(solution)/shard_map/ppermute | solution.py:18
  774.3 171.2 %copy-start.3 = (bf16[64,4,8,128]{3,0,2,1:T(8,128)(2,1)S(1)}, bf16[64,4,8,128]{3,0,2,1:T(8,128)(2,1)}, u32[]{:S(2)}) copy-start(bf16[64,4,8,128]{3,0,2,1:T(8,128)(2,1)} %copy.168) | copy-start | bytes 1572868
  1089.7 41.0 %collective-permute-start.14 = (bf16[256,1024]{1,0:T(8,128)(2,1)S(1)}, bf16[256,1024]{1,0:T(8,128)(2,1)S(1)}, u32[]{:S(2)}, u32[]{:S(2)}) collective-permute-start(bf16[256,1024]{1,0:T(8,128)(2,1)S(1)} %get-tuple-element.3566), channel_id=1, source_target_pairs={{1,0},{2,1},{3,2},{4,3},{5,4},{6,5},{7,6},{8,7},{9,8},{10,9},{11,1... | collective-permute-start | bytes 1572872 | tf_op jit(solution)/shard_map/ppermute | solution.py:18
  1123.9 15.6 %collective-permute-start.21 = (bf16[256,1024]{1,0:T(8,128)(2,1)S(1)}, bf16[256,1024]{1,0:T(8,128)(2,1)S(1)}, u32[]{:S(2)}, u32[]{:S(2)}) collective-permute-start(bf16[256,1024]{1,0:T(8,128)(2,1)S(1)} %get-tuple-element.3567), channel_id=1, source_target_pairs={{0,1},{1,2},{2,3},{3,4},{4,5},{5,6},{6,7},{7,8},{8,9},{9,10},{10,1... | collective-permute-start | bytes 1572872 | tf_op jit(solution)/shard_map/ppermute | solution.py:18
  1141.5 12.6 collective-permute-start.15
  1146.0 15.7 %collective-permute-start.22 = (bf16[256,1024]{1,0:T(8,128)(2,1)S(1)}, bf16[256,1024]{1,0:T(8,128)(2,1)}, u32[]{:S(2)}, u32[]{:S(2)}) collective-permute-start(bf16[256,1024]{1,0:T(8,128)(2,1)S(1)} %get-tuple-element.3565), channel_id=1, source_target_pairs={{0,1},{1,2},{2,3},{3,4},{4,5},{5,6},{6,7},{7,8},{8,9},{9,10},{10,1... | collective-permute-start | bytes 1572872 | tf_op jit(solution)/shard_map/ppermute | solution.py:18
  1163.8 12.6 collective-permute-start.16
  1168.3 15.6 %collective-permute-start.23 = (bf16[256,1024]{1,0:T(8,128)(2,1)S(1)}, bf16[256,1024]{1,0:T(8,128)(2,1)S(1)}, u32[]{:S(2)}, u32[]{:S(2)}) collective-permute-start(bf16[256,1024]{1,0:T(8,128)(2,1)S(1)} %get-tuple-element.3563), channel_id=1, source_target_pairs={{0,1},{1,2},{2,3},{3,4},{4,5},{5,6},{6,7},{7,8},{8,9},{9,10},{10,1... | collective-permute-start | bytes 1572872 | tf_op jit(solution)/shard_map/ppermute | solution.py:18
  1185.9 12.6 collective-permute-start.17
  1190.4 15.6 %collective-permute-start.24 = (bf16[256,1024]{1,0:T(8,128)(2,1)S(1)}, bf16[256,1024]{1,0:T(8,128)(2,1)S(1)}, u32[]{:S(2)}, u32[]{:S(2)}) collective-permute-start(bf16[256,1024]{1,0:T(8,128)(2,1)S(1)} %get-tuple-element.3561), channel_id=1, source_target_pairs={{0,1},{1,2},{2,3},{3,4},{4,5},{5,6},{6,7},{7,8},{8,9},{9,10},{10,1... | collective-permute-start | bytes 1572872 | tf_op jit(solution)/shard_map/ppermute | solution.py:18
  1207.9 12.6 collective-permute-start.18
  1212.5 15.6 %collective-permute-start.25 = (bf16[256,1024]{1,0:T(8,128)(2,1)S(1)}, bf16[256,1024]{1,0:T(8,128)(2,1)S(1)}, u32[]{:S(2)}, u32[]{:S(2)}) collective-permute-start(bf16[256,1024]{1,0:T(8,128)(2,1)S(1)} %get-tuple-element.3559), channel_id=1, source_target_pairs={{0,1},{1,2},{2,3},{3,4},{4,5},{5,6},{6,7},{7,8},{8,9},{9,10},{10,1... | collective-permute-start | bytes 1572872 | tf_op jit(solution)/shard_map/ppermute | solution.py:18
  1218.1 21.4 %copy-start.9 = (bf16[64,4,8,128]{3,0,2,1:T(8,128)(2,1)S(1)}, bf16[64,4,8,128]{3,0,2,1:T(8,128)(2,1)}, u32[]{:S(2)}) copy-start(bf16[64,4,8,128]{3,0,2,1:T(8,128)(2,1)} %get-tuple-element.3507) | copy-start | bytes 1572868
  1218.1 22.0 %copy-start.8 = (bf16[64,4,8,128]{3,0,2,1:T(8,128)(2,1)S(1)}, bf16[64,4,8,128]{3,0,2,1:T(8,128)(2,1)}, u32[]{:S(2)}) copy-start(bf16[64,4,8,128]{3,0,2,1:T(8,128)(2,1)} %get-tuple-element.3509) | copy-start | bytes 1572868
  1230.0 12.7 collective-permute-start.19
  1234.7 15.6 %collective-permute-start.26 = (bf16[256,1024]{1,0:T(8,128)(2,1)S(1)}, bf16[256,1024]{1,0:T(8,128)(2,1)S(1)}, u32[]{:S(2)}, u32[]{:S(2)}) collective-permute-start(bf16[256,1024]{1,0:T(8,128)(2,1)S(1)} %get-tuple-element.3557), channel_id=1, source_target_pairs={{0,1},{1,2},{2,3},{3,4},{4,5},{5,6},{6,7},{7,8},{8,9},{9,10},{10,1... | collective-permute-start | bytes 1572872 | tf_op jit(solution)/shard_map/ppermute | solution.py:18
  1252.3 15.8 %collective-permute-start.27 = (bf16[256,1024]{1,0:T(8,128)(2,1)S(1)}, bf16[256,1024]{1,0:T(8,128)(2,1)S(1)}, u32[]{:S(2)}, u32[]{:S(2)}) collective-permute-start(bf16[256,1024]{1,0:T(8,128)(2,1)S(1)} %get-tuple-element.3555), channel_id=1, source_target_pairs={{0,1},{1,2},{2,3},{3,4},{4,5},{5,6},{6,7},{7,8},{8,9},{9,10},{10,1... | collective-permute-start | bytes 1572872 | tf_op jit(solution)/shard_map/ppermute | solution.py:18
  1254.2 18.2 %collective-permute-start.20 = (bf16[256,1024]{1,0:T(8,128)(2,1)S(1)}, bf16[256,1024]{1,0:T(8,128)(2,1)S(1)}, u32[]{:S(2)}, u32[]{:S(2)}) collective-permute-start(bf16[256,1024]{1,0:T(8,128)(2,1)S(1)} %get-tuple-element.3554), channel_id=1, source_target_pairs={{1,0},{2,1},{3,2},{4,3},{5,4},{6,5},{7,6},{8,7},{9,8},{10,9},{11,1... | collective-permute-start | bytes 1572872 | tf_op jit(solution)/shard_map/ppermute | solution.py:18
  (11 other events, 77.5 us)
where the time goes:
time: 1300 us; the launch traced here: 1280 us
  other arithmetic  301 us (23%)
  matrix products  254 us (20%)
  local copies, waits for them, and re-layouts  225 us (17%)
  starting transfers between devices  165 us (13%)
  loops' own time  135 us (10%)
  waiting for transfers between devices  116 us (9%)
  blocking collectives  73.1 us (6%)
    ppermute x28, starting transfers between devices, passed_along(): lax.ppermute(value, axis, [(source, source + steps) for source in range(l...  165 us
    ppermute x28, waiting for transfers between devices, passed_along(): lax.ppermute(value, axis, [(source, source + steps) for source in range(l...  116 us
    squeeze x102, local copies, waits for them, and re-layouts, block_parts(): lax.dynamic_index_in_dim(key_blocks, block_index, 0, keepdims=False)  99.4 us
    dot_general x34, matrix products, backward_attend(): jnp.einsum('kgqs,skd->qkgd', dscore, keys_part, preferred_element_type=jn...  85.7 us
    psum x1, blocking collectives, on_device(): weight_sum = lax.psum(jnp.sum(token_weight), ('dp', 'cp'))  73.1 us
    dynamic_update_slice x34, other arithmetic, backward_attend(): lax.dynamic_update_index_in_dim(dkv_sum, current + update, block_index, 0)  66.3 us
    dot_general x34, matrix products, attend_attend(): jnp.einsum('kgqs,skd->qkgd', probs.astype(jnp.bfloat16), values_part, pre...  63.2 us
    reduce_or x64, other arithmetic, attend_visit_block(): jnp.any(visible)  45.9 us
  transfers between devices with their start and end apart: 28, of which 19 were waited for; matrix products, arithmetic and copies ran while one was open for 5% of the time, Pallas kernels for 0%

commit v1 on v0

v1 whole, which is shorter than its diff:
```python
import functools

import jax
import jax.numpy as jnp
from jax import lax
from jax.experimental import pallas as pl
from jax.experimental.pallas import tpu as pltpu
from jax.sharding import PartitionSpec as P

HEADS = 32
KV_HEADS = 4
HEAD_DIM = 128
SPAN_MAX = 8
HALF = 128
ROWS_DEV = 256
SLOTS = 8
GROUPS = HEADS // KV_HEADS
TILES = GROUPS // 2
PAIR = 256
VISITS = 9
NEG = -1e30
SCALE = HEAD_DIM**-0.5
SCALE_LOG2 = SCALE * 1.4426950408889634
F32 = jnp.float32
BF16 = jnp.bfloat16


def dot(a, b):
    return lax.dot_general(a, b, (((1,), (0,)), ((), ())), preferred_element_type=F32)


def dot_nt(a, b):
    return lax.dot_general(a, b, (((1,), (1,)), ((), ())), preferred_element_type=F32)


def kernel(
    n_dp,
    n_blocks,
    q_ref,
    k_ref,
    v_ref,
    g_ref,
    w_ref,
    span_ref,
    len_ref,
    o_ref,
    dq_ref,
    dk_ref,
    dv_ref,
    kv,
    stage,
    inbox,
    own_acc,
    q_t,
    d_t,
    dout,
    bias,
    s_scr,
    p_scr,
    acc,
    row_max,
    row_sum,
    o_acc,
    dq_acc,
    delta,
    qt_scaled,
    dt_scaled,
    sum_block,
    sum_dp,
    sum_y,
    kv_send,
    kv_recv,
    st_send,
    st_recv,
    w_send,
    w_recv,
):
    dp = lax.axis_index("dp")
    cp = lax.axis_index("cp")
    me = lax.rem(cp, SPAN_MAX)
    block = lax.div(cp, SPAN_MAX)
    base = block * SPAN_MAX
    half_me = lax.div(me, 2)
    odd = lax.rem(me, 2)

    def peer_of(step):
        return lax.rem(me + step, SPAN_MAX)

    def at_member(member):
        return (dp, base + member)

    def at_dp(step):
        return (lax.rem(dp + step, n_dp), cp)

    def at_block(step):
        return (dp, lax.rem(block + step, n_blocks) * SPAN_MAX + me)

    barrier = pltpu.get_barrier_semaphore()
    partners = [at_member(peer_of(step)) for step in range(1, SPAN_MAX)]
    partners += [at_dp(step) for step in range(1, n_dp)]
    partners += [at_block(step) for step in range(1, n_blocks)]
    for partner in partners:
        pl.semaphore_signal(barrier, inc=1, device_id=partner, device_id_type=pl.DeviceIdType.MESH)

    def rows_at(half, member):
        return pl.ds(pl.multiple_of((half * SPAN_MAX + member) * HALF, HALF), HALF)

    for head in range(KV_HEADS):
        lanes = slice(head * HEAD_DIM, (head + 1) * HEAD_DIM)
        for half in range(2):
            rows = slice(half * HALF, (half + 1) * HALF)
            kv[head, rows_at(half, me), 0:HEAD_DIM] = k_ref[rows, lanes]
            kv[head, rows_at(half, me), HEAD_DIM : 2 * HEAD_DIM] = v_ref[rows, lanes]

    weight_part = jnp.sum(w_ref[...], axis=1, keepdims=True)
    sum_block[me] = jnp.broadcast_to(weight_part, (8, 128))

    pl.semaphore_wait(barrier, len(partners))

    def remote(src, dst, send_sem, recv_sem, target):
        return pltpu.make_async_remote_copy(
            src_ref=src,
            dst_ref=dst,
            send_sem=send_sem,
            recv_sem=recv_sem,
            device_id=target,
            device_id_type=pl.DeviceIdType.MESH,
        )

    def weight_copy(buffer, slot, offset, step, target, source_slot):
        return remote(
            buffer.at[slot],
            buffer.at[slot],
            w_send.at[offset + step - 1],
            w_recv.at[offset + source_slot],
            target,
        )

    def send_weights(buffer, slot, count, offset, targets):
        for step in range(1, count):
            weight_copy(buffer, slot, offset, step, targets(step), slot).start()

    def wait_weights(buffer, slot, count, offset, targets):
        for step in range(1, count):
            source = lax.rem(slot + step, count)
            weight_copy(buffer, source, offset, step, targets(step), source).wait_recv()
            weight_copy(buffer, slot, offset, step, targets(step), slot).wait_send()
        total = buffer[0]
        for slot_index in range(1, count):
            total = total + buffer[slot_index]
        return total

    def kv_copy(head, half, source, target):
        return remote(
            kv.at[head, rows_at(half, source)],
            kv.at[head, rows_at(half, source)],
            kv_send.at[head, half, target],
            kv_recv.at[head, half, source],
            at_member(target),
        )

    def upper_needed(source, target):
        return (source > target) | ((lax.rem(target, 2) == 1) & (source == target - 1))

    send_weights(sum_block, me, SPAN_MAX, 0, lambda step: at_member(peer_of(step)))

    def send_kv(head, carry):
        for step in range(1, SPAN_MAX):
            peer = peer_of(step)
            kv_copy(head, 0, me, peer).start()

            @pl.when(upper_needed(me, peer))
            def _():
                kv_copy(head, 1, me, peer).start()

        return carry

    lax.fori_loop(0, KV_HEADS, send_kv, 0)

    span = span_ref[0, cp]
    spread = span > 1
    row_id = lax.broadcasted_iota(jnp.int32, (HALF, HALF), 0)
    col_id = lax.broadcasted_iota(jnp.int32, (HALF, HALF), 1)
    slot_of = {}
    for name, ids in (("q0", row_id), ("q1", row_id + HALF), ("k0", col_id), ("k1", col_id + HALF)):
        slot_count = jnp.zeros((HALF, HALF), jnp.int32)
        end = jnp.int32(0)
        for slot in range(SLOTS):
            end = end + len_ref[0, cp, slot]
            slot_count = slot_count + (ids >= end).astype(jnp.int32)
        slot_of[name] = slot_count
    spread_add = jnp.where(spread, 1, 0)

    def same_document(q_name, k_name):
        equal = (slot_of[q_name] == slot_of[k_name]).astype(jnp.int32) + spread_add
        return jnp.where(equal > 0, 0.0, NEG)

    causal = jnp.where(col_id <= row_id, 0.0, NEG)
    own_lower = jnp.minimum(same_document("q0", "k0"), causal)
    own_upper = jnp.minimum(same_document("q1", "k1"), causal)
    own_cross = same_document("q1", "k0")

    def member_bias(member, keep, own):
        seen = jnp.where((lax.bitwise_xor(member, me) < span) & keep, 0.0, NEG)
        is_me = jnp.where(member == me, 1, 0)
        return jnp.where(is_me + jnp.zeros((HALF, HALF), jnp.int32) > 0, own, seen)

    for visit in range(VISITS):
        for side in range(2):
            lanes = slice(side * HALF, (side + 1) * HALF)
            if visit < 4:
                member = jnp.int32(2 * visit + side)
                bias[visit, :, lanes] = member_bias(member, member >= 0, own_cross)
            else:
                extra = visit - 4
                low = member_bias(jnp.int32(2 * extra + side), 2 * extra + side < me, own_lower)
                high = member_bias(jnp.int32(2 * extra - 2 + side), 2 * extra - 2 + side > me, own_upper)
                is_low = jnp.where(extra <= half_me, 1, 0)
                bias[visit, :, lanes] = jnp.where(
                    is_low + jnp.zeros((HALF, HALF), jnp.int32) > 0, low, high
                )

    def turn_queries(index, carry):
        for head in range(2):
            lanes = pl.ds(pl.multiple_of((index * 2 + head) * HEAD_DIM, HEAD_DIM), HEAD_DIM)
            for half in range(2):
                part = q_ref[half * HALF : (half + 1) * HALF, lanes]
                q_t[index, half, :, head * HALF : (head + 1) * HALF] = part.T
        return carry

    lax.fori_loop(0, HEADS // 2, turn_queries, 0)

    block_sum = wait_weights(sum_block, me, SPAN_MAX, 0, lambda step: at_member(peer_of(step)))
    sum_dp[dp] = block_sum
    send_weights(sum_dp, dp, n_dp, 8, at_dp)
    dp_sum = wait_weights(sum_dp, dp, n_dp, 8, at_dp)
    sum_y[block] = dp_sum
    send_weights(sum_y, block, n_blocks, 16, at_block)
    weight_sum = wait_weights(sum_y, block, n_blocks, 16, at_block)
    rows_total = ROWS_DEV * SPAN_MAX * n_dp * n_blocks
    inverse_mean = rows_total / weight_sum[0:1, :]

    for half in range(2):
        rows = slice(half * HALF, (half + 1) * HALF)
        scaled = jnp.broadcast_to(w_ref[0:1, rows] * inverse_mean, (HALF, HALF)).T

        def weigh(index, carry, rows=rows, half=half, scaled=scaled):
            for head in range(2):
                lanes = pl.ds(pl.multiple_of((index * 2 + head) * HEAD_DIM, HEAD_DIM), HEAD_DIM)
                part = (g_ref[rows, lanes].astype(F32) * scaled).astype(BF16)
                dout[rows, lanes] = part
                d_t[index, half, :, head * HALF : (head + 1) * HALF] = part.T
            return carry

        lax.fori_loop(0, HEADS // 2, weigh, 0)

    def half_of(visit):
        if visit < 4 or visit == 8:
            return 1
        if visit == 4:
            return 0
        return jnp.where(visit - 4 <= half_me, 0, 1)

    def pair_of(visit):
        if visit < 4:
            return visit
        if visit == 4:
            return 0
        if visit == 8:
            return 7
        return jnp.where(visit - 4 <= half_me, visit - 4, visit - 1)

    def tile_step(head, tile):
        index = head * TILES + tile

        def lanes_of(part):
            return pl.ds(pl.multiple_of((index * 2 + part) * HEAD_DIM, HEAD_DIM), HEAD_DIM)

        def tall(ref, half):
            rows = pl.ds(half * HALF, HALF) if isinstance(half, int) else pl.ds(pl.multiple_of(half * HALF, HALF), HALF)
            return jnp.concatenate([ref[rows, lanes_of(0)], ref[rows, lanes_of(1)]], axis=0)

        def pair_rows(visit):
            pair = pair_of(visit)
            if isinstance(pair, int):
                return pl.ds(pair * PAIR, PAIR)
            return pl.ds(pl.multiple_of(pair * PAIR, PAIR), PAIR)

        row_max[...] = jnp.full(row_max.shape, NEG, F32)
        row_sum[...] = jnp.zeros(row_sum.shape, F32)
        o_acc[...] = jnp.zeros(o_acc.shape, F32)
        dq_acc[...] = jnp.zeros(dq_acc.shape, F32)

        for visit in range(VISITS):
            half = half_of(visit)
            keys = kv[head, pair_rows(visit), 0:HEAD_DIM]
            masked = bias[visit]
            scores = dot_nt(tall(q_ref, half), keys) * SCALE_LOG2 + jnp.concatenate([masked, masked], axis=0)
            s_scr[visit] = scores
            row_max[half] = jnp.maximum(
                row_max[half], jnp.maximum(scores[:, :HALF], scores[:, HALF:])
            )
        for half in range(2):
            row_max[half] = jnp.broadcast_to(
                jnp.max(row_max[half], axis=1, keepdims=True), (PAIR, HALF)
            )
        for visit in range(VISITS):
            half = half_of(visit)
            values = kv[head, pair_rows(visit), HEAD_DIM : 2 * HEAD_DIM]
            top = row_max[half]
            probs = jnp.exp2(s_scr[visit] - jnp.concatenate([top, top], axis=1))
            row_sum[half] = row_sum[half] + (probs[:, :HALF] + probs[:, HALF:])
            probs = probs.astype(BF16)
            p_scr[visit] = probs
            o_acc[half] = o_acc[half] + dot(probs, values)
        for half in range(2):
            total = jnp.sum(row_sum[half], axis=1, keepdims=True)
            inverse = jnp.broadcast_to(1.0 / total, (PAIR, HALF))
            row_sum[half] = inverse
            out = (o_acc[half] * inverse).astype(BF16)
            rows = slice(half * HALF, (half + 1) * HALF)
            o_ref[rows, lanes_of(0)] = out[:HALF]
            o_ref[rows, lanes_of(1)] = out[HALF:]
            product = tall(dout, half).astype(F32) * out.astype(F32)
            delta[half] = jnp.broadcast_to(jnp.sum(product, axis=1, keepdims=True), (PAIR, HALF))
            turned = jnp.concatenate([inverse[:HALF].T, inverse[HALF:].T], axis=1)
            qt_scaled[half] = (q_t[index, half].astype(F32) * turned).astype(BF16)
            dt_scaled[half] = (d_t[index, half].astype(F32) * turned).astype(BF16)
        for visit in range(VISITS):
            half = half_of(visit)
            pair = pair_of(visit)
            keys = kv[head, pair_rows(visit), 0:HEAD_DIM]
            values = kv[head, pair_rows(visit), HEAD_DIM : 2 * HEAD_DIM]
            dprobs = dot_nt(tall(dout, half), values)
            shift = delta[half]
            probs = p_scr[visit]
            dscore = probs.astype(F32) * (dprobs - jnp.concatenate([shift, shift], axis=1))
            dscore = dscore.astype(BF16)
            dq_acc[half] = dq_acc[half] + dot(dscore, keys)
            acc[pair, 0:HEAD_DIM] = acc[pair, 0:HEAD_DIM] + dot(qt_scaled[half], dscore)
            acc[pair, HEAD_DIM : 2 * HEAD_DIM] = acc[pair, HEAD_DIM : 2 * HEAD_DIM] + dot(
                dt_scaled[half], probs
            )
        for half in range(2):
            result = (dq_acc[half] * (row_sum[half] * SCALE)).astype(BF16)
            rows = slice(half * HALF, (half + 1) * HALF)
            dq_ref[rows, lanes_of(0)] = result[:HALF]
            dq_ref[rows, lanes_of(1)] = result[HALF:]

    def stage_copy(head, half, source, target):
        return remote(
            stage.at[head, half, target],
            inbox.at[head, half, source],
            st_send.at[head, half, target],
            st_recv.at[head, half, source],
            at_member(target),
        )

    def head_step(head, carry):
        for step in range(1, SPAN_MAX):
            peer = peer_of(step)
            kv_copy(head, 0, peer, peer).wait_recv()

            @pl.when(upper_needed(peer, me))
            def _():
                kv_copy(head, 1, peer, peer).wait_recv()

        acc[...] = jnp.zeros(acc.shape, F32)

        def inner(tile, inner_carry):
            tile_step(head, tile)
            return inner_carry

        lax.fori_loop(0, TILES, inner, 0)
        for half in range(2):
            for member in range(SPAN_MAX):
                lanes = slice((member % 2) * HALF, (member % 2 + 1) * HALF)
                part = acc[half * 4 + member // 2, :, lanes]
                stage[head, half, member] = part.astype(BF16)

                @pl.when(member == me)
                def _():
                    own_acc[head, half] = part

        for step in range(1, SPAN_MAX):
            peer = peer_of(step)
            stage_copy(head, 0, me, peer).start()

            @pl.when(peer > me)
            def _():
                stage_copy(head, 1, me, peer).start()

        return carry

    lax.fori_loop(0, KV_HEADS, head_step, 0)

    def finish(head, carry):
        lanes = pl.ds(pl.multiple_of(head * HEAD_DIM, HEAD_DIM), HEAD_DIM)
        for step in range(1, SPAN_MAX):
            peer = peer_of(step)
            stage_copy(head, 0, peer, peer).wait_recv()
            own_acc[head, 0] = own_acc[head, 0] + inbox[head, 0, peer].astype(F32)

            @pl.when(peer < me)
            def _():
                stage_copy(head, 1, peer, peer).wait_recv()
                own_acc[head, 1] = own_acc[head, 1] + inbox[head, 1, peer].astype(F32)

        for half in range(2):
            rows = slice(half * HALF, (half + 1) * HALF)
            dk_ref[rows, lanes] = (own_acc[head, half, 0:HEAD_DIM] * SCALE).T.astype(BF16)
            dv_ref[rows, lanes] = own_acc[head, half, HEAD_DIM : 2 * HEAD_DIM].T.astype(BF16)
        for step in range(1, SPAN_MAX):
            peer = peer_of(step)
            kv_copy(head, 0, me, peer).wait_send()
            stage_copy(head, 0, me, peer).wait_send()

            @pl.when(upper_needed(me, peer))
            def _():
                kv_copy(head, 1, me, peer).wait_send()

            @pl.when(peer > me)
            def _():
                stage_copy(head, 1, me, peer).wait_send()

        return carry

    lax.fori_loop(0, KV_HEADS, finish, 0)


def on_device(n_dp, n_blocks, queries, key_states, value_states, grad_out, token_weight, span_size, short_lengths):
    vmem = pl.BlockSpec(memory_space=pltpu.VMEM)
    smem = pl.BlockSpec(memory_space=pltpu.SMEM)
    wide = jax.ShapeDtypeStruct((ROWS_DEV, HEADS * HEAD_DIM), BF16)
    narrow = jax.ShapeDtypeStruct((ROWS_DEV, KV_HEADS * HEAD_DIM), BF16)
    tile = (2, PAIR, HALF)
    return pl.pallas_call(
        functools.partial(kernel, n_dp, n_blocks),
        out_shape=(wide, wide, narrow, narrow),
        in_specs=[vmem] * 5 + [smem] * 2,
        out_specs=(vmem,) * 4,
        scratch_shapes=[
            pltpu.VMEM((KV_HEADS, 2 * SPAN_MAX * HALF, 2 * HEAD_DIM), BF16),
            pltpu.VMEM((KV_HEADS, 2, SPAN_MAX, 2 * HEAD_DIM, HALF), BF16),
            pltpu.VMEM((KV_HEADS, 2, SPAN_MAX, 2 * HEAD_DIM, HALF), BF16),
            pltpu.VMEM((KV_HEADS, 2, 2 * HEAD_DIM, HALF), F32),
            pltpu.VMEM((HEADS // 2, 2, HEAD_DIM, PAIR), BF16),
            pltpu.VMEM((HEADS // 2, 2, HEAD_DIM, PAIR), BF16),
            pltpu.VMEM((ROWS_DEV, HEADS * HEAD_DIM), BF16),
            pltpu.VMEM((VISITS, HALF, PAIR), F32),
            pltpu.VMEM((VISITS, PAIR, PAIR), F32),
            pltpu.VMEM((VISITS, PAIR, PAIR), BF16),
            pltpu.VMEM((SPAN_MAX, 2 * HEAD_DIM, PAIR), F32),
            pltpu.VMEM(tile, F32),
            pltpu.VMEM(tile, F32),
            pltpu.VMEM(tile, F32),
            pltpu.VMEM(tile, F32),
            pltpu.VMEM(tile, F32),
            pltpu.VMEM((2, HEAD_DIM, PAIR), BF16),
            pltpu.VMEM((2, HEAD_DIM, PAIR), BF16),
            pltpu.VMEM((SPAN_MAX, 8, 128), F32),
            pltpu.VMEM((n_dp, 8, 128), F32),
            pltpu.VMEM((n_blocks, 8, 128), F32),
            pltpu.SemaphoreType.DMA((KV_HEADS, 2, SPAN_MAX)),
            pltpu.SemaphoreType.DMA((KV_HEADS, 2, SPAN_MAX)),
            pltpu.SemaphoreType.DMA((KV_HEADS, 2, SPAN_MAX)),
            pltpu.SemaphoreType.DMA((KV_HEADS, 2, SPAN_MAX)),
            pltpu.SemaphoreType.DMA((24,)),
            pltpu.SemaphoreType.DMA((24,)),
        ],
        compiler_params=pltpu.CompilerParams(
            collective_id=0, has_side_effects=True, vmem_limit_bytes=56 * 1024 * 1024
        ),
    )(
        queries,
        key_states,
        value_states,
        grad_out,
        token_weight.reshape(1, ROWS_DEV),
        span_size,
        short_lengths,
    )


def solution(mesh):
    rows = P(("dp", "cp"), None)
    n_dp = mesh.shape["dp"]
    n_blocks = mesh.shape["cp"] // SPAN_MAX
    return jax.shard_map(
        functools.partial(on_device, n_dp, n_blocks),
        mesh=mesh,
        in_specs=(rows, rows, rows, rows, P(("dp", "cp")), P("dp", None), P("dp", None, None)),
        out_specs=(rows, rows, rows, rows),
        check_vma=False,
    )
```

time: 1300 us -> 150 us (0.12)
  the two profiles are of different devices: /device:TPU:8 before, /device:TPU:0 now
where the time goes in v1:
time: 150 us; the launch traced here: 147 us
  Pallas kernels  139 us (93%)
  local copies, waits for them, and re-layouts  7.38 us (5%)
    pallas_call x1, Pallas kernels, on_device(): pl.pallas_call(functools.partial(kernel, n_dp, n_blocks), out_shape=(wide...  139 us
    unnamed x11, local copies, waits for them, and re-layouts  7.38 us

profile of v1, /device:TPU:0, one launch (start us, length us, event | category | flops | bytes accessed | tf_op | source)
XLA Modules:
  0.0 147.0 jit_solution(4753372070870569277)
XLA Ops:
  0.6 1.4 copy.11.len_ref
  2.0 138.9 %shard_map.102 = (bf16[256,4096]{1,0:T(8,128)(2,1)}, bf16[256,4096]{1,0:T(8,128)(2,1)}, bf16[256,512]{1,0:T(8,128)(2,1)}, bf16[256,512]{1,0:T(8,128)(2,1)}) custom-call(bf16[256,4096]{1,0:T(8,128)(2,1)} %q_ref.1, bf16[256,512]{1,0:T(8,128)(2,1)} %k_ref.1, bf16[256,512]{1,0:T(8,128)(2,1)} %v_ref.1, bf16[256,4096]{1,0:T(8,128)(2,1)} %g_ref.1, ...), custom_call_target="tpu_custom_call" | custom-call | tf_op jit(solution)/shard_map/pallas_call | solution.py:437
  140.9 0.0 copy-start
  140.9 3.3 %copy.16 = bf16[256,4096]{1,0:T(8,128)(2,1)} copy(bf16[256,4096]{1,0:T(8,128)(2,1)} %get-tuple-element.8) | data formatting | bytes 4194304
  144.2 0.0 copy-done
  144.2 0.0 copy-start.2
  144.2 0.0 copy-start.1
  144.2 1.3 copy.17
  145.6 0.0 copy-done.2
  145.6 0.7 copy.18
  146.3 0.0 copy-done.1
  146.3 0.7 copy.19
Async XLA Ops:
  140.9 3.3 %copy-start = (bf16[256,4096]{1,0:T(8,128)(2,1)S(1)}, bf16[256,4096]{1,0:T(8,128)(2,1)}, u32[]{:S(2)}) copy-start(bf16[256,4096]{1,0:T(8,128)(2,1)} %get-tuple-element.9) | copy-start | bytes 6291460
  144.2 1.3 copy-start.2
  144.2 2.0 %copy-start.1 = (bf16[256,512]{1,0:T(8,128)(2,1)S(1)}, bf16[256,512]{1,0:T(8,128)(2,1)}, u32[]{:S(2)}) copy-start(bf16[256,512]{1,0:T(8,128)(2,1)} %get-tuple-element.11) | copy-start | bytes 786436

commit v2 on v1

v2 whole, which is shorter than its diff:
```python
import functools

import jax
import jax.numpy as jnp
from jax import lax
from jax.experimental import pallas as pl
from jax.experimental.pallas import tpu as pltpu
from jax.sharding import PartitionSpec as P

HEADS = 32
KV_HEADS = 4
HEAD_DIM = 128
SPAN_MAX = 8
HALF = 128
ROWS_DEV = 256
SLOTS = 8
GROUPS = HEADS // KV_HEADS
TILES = GROUPS // 2
PAIR = 256
VISITS = 9
FORWARD_ORDER = (1, 3, 5, 0, 2, 4, 6, 7, 8)
NEG = -1e30
SCALE = HEAD_DIM**-0.5
SCALE_LOG2 = SCALE * 1.4426950408889634
F32 = jnp.float32
BF16 = jnp.bfloat16


def dot(a, b):
    return lax.dot_general(a, b, (((1,), (0,)), ((), ())), preferred_element_type=F32)


def dot_nt(a, b):
    return lax.dot_general(a, b, (((1,), (1,)), ((), ())), preferred_element_type=F32)


def kernel(
    n_dp,
    n_blocks,
    q_hbm,
    k_ref,
    v_ref,
    g_hbm,
    w_ref,
    span_ref,
    len_ref,
    o_hbm,
    dq_hbm,
    dk_ref,
    dv_ref,
    q_ref,
    g_ref,
    o_ref,
    dq_ref,
    kv,
    first_out,
    first_in,
    second_out,
    second_in,
    last_out,
    last_in,
    cross_out,
    cross_in,
    owed_out,
    owed_in,
    q_t,
    d_t,
    dout,
    bias,
    s_scr,
    p_scr,
    acc,
    row_max,
    o_fold,
    dq_acc,
    delta,
    inverses,
    qt_scaled,
    dt_scaled,
    sum_block,
    sum_dp,
    sum_y,
    inverse_mean,
    in_sem,
    out_sem,
    z_send,
    z_recv,
    near_send,
    near_recv,
    far_send,
    far_recv,
    up_send,
    up_recv,
    turn_send,
    turn_recv,
    first_send,
    first_recv,
    second_send,
    second_recv,
    last_send,
    last_recv,
    cross_send,
    cross_recv,
    owed_send,
    owed_recv,
    w_send,
    w_recv,
):
    dp = lax.axis_index("dp")
    cp = lax.axis_index("cp")
    me = lax.rem(cp, SPAN_MAX)
    block = lax.div(cp, SPAN_MAX)
    base = block * SPAN_MAX
    half_me = lax.div(me, 2)
    odd = lax.rem(me, 2)

    def peer_of(step):
        return lax.rem(me + step, SPAN_MAX)

    def at_member(member):
        return (dp, base + member)

    def at_dp(step):
        return (lax.rem(dp + step, n_dp), cp)

    def at_block(step):
        return (dp, lax.rem(block + step, n_blocks) * SPAN_MAX + me)

    barrier = pltpu.get_barrier_semaphore()
    partners = [at_member(peer_of(step)) for step in range(1, SPAN_MAX)]
    partners += [at_dp(step) for step in range(1, n_dp)]
    partners += [at_block(step) for step in range(1, n_blocks)]
    for partner in partners:
        pl.semaphore_signal(barrier, inc=1, device_id=partner, device_id_type=pl.DeviceIdType.MESH)

    across = lax.rem(half_me + 2, 4)
    left = lax.rem(half_me + 3, 4)
    right = lax.rem(half_me + 1, 4)
    own_rows = pl.ds(pl.multiple_of(odd * HALF, HALF), HALF)
    other_rows = pl.ds(pl.multiple_of((1 - odd) * HALF, HALF), HALF)

    def head_lanes(head):
        width = GROUPS * HEAD_DIM
        return pl.ds(pl.multiple_of(head * width, width), width)

    def load_queries(head):
        return pltpu.make_async_copy(
            q_hbm.at[:, head_lanes(head)], q_ref.at[:, head_lanes(head)], in_sem.at[0, head]
        )

    def load_grads(head):
        return pltpu.make_async_copy(
            g_hbm.at[:, head_lanes(head)], g_ref.at[:, head_lanes(head)], in_sem.at[1, head]
        )

    def save_out(head):
        return pltpu.make_async_copy(
            o_ref.at[:, head_lanes(head)], o_hbm.at[:, head_lanes(head)], out_sem.at[0, head]
        )

    def save_dquery(head):
        return pltpu.make_async_copy(
            dq_ref.at[:, head_lanes(head)], dq_hbm.at[:, head_lanes(head)], out_sem.at[1, head]
        )

    for head in range(KV_HEADS):
        load_queries(head).start()
        load_grads(head).start()

    for head in range(KV_HEADS):
        lanes = slice(head * HEAD_DIM, (head + 1) * HEAD_DIM)
        for half in range(2):
            rows = slice(half * HALF, (half + 1) * HALF)
            kv[head, half_me, half, own_rows, 0:HEAD_DIM] = k_ref[rows, lanes]
            kv[head, half_me, half, own_rows, HEAD_DIM : 2 * HEAD_DIM] = v_ref[rows, lanes]

    weight_part = jnp.sum(w_ref[...], axis=1, keepdims=True)
    sum_block[me] = jnp.broadcast_to(weight_part, (8, 128))

    pl.semaphore_wait(barrier, len(partners))

    def remote(src, dst, send_sem, recv_sem, target):
        return pltpu.make_async_remote_copy(
            src_ref=src,
            dst_ref=dst,
            send_sem=send_sem,
            recv_sem=recv_sem,
            device_id=target,
            device_id_type=pl.DeviceIdType.MESH,
        )

    def weight_copy(buffer, slot, offset, step, target, source_slot):
        return remote(
            buffer.at[slot],
            buffer.at[slot],
            w_send.at[offset + step - 1],
            w_recv.at[offset + source_slot],
            target,
        )

    def send_weights(buffer, slot, count, offset, targets):
        for step in range(1, count):
            weight_copy(buffer, slot, offset, step, targets(step), slot).start()

    def wait_weights(buffer, slot, count, offset, targets):
        for step in range(1, count):
            source = lax.rem(slot + step, count)
            weight_copy(buffer, source, offset, step, targets(step), source).wait_recv()
            weight_copy(buffer, slot, offset, step, targets(step), slot).wait_send()
        total = buffer[0]
        for slot_index in range(1, count):
            total = total + buffer[slot_index]
        return total

    partner_at = at_member(lax.bitwise_xor(me, 1))
    left_at = at_member(left * 2 + odd)
    right_at = at_member(right * 2 + odd)

    def rows_of(item):
        return own_rows if item == 0 else other_rows

    def when(condition, step, *given):
        @pl.when(condition)
        def _():
            step(*given)

    sides = (left_at, right_at)

    def partner_copy(head):
        view = kv.at[head, half_me, 0, own_rows]
        return remote(view, view, z_send.at[head], z_recv.at[head], partner_at)

    def near_copy(head, item, way, pair):
        view = kv.at[head, pair, 0, rows_of(item)]
        return remote(view, view, near_send.at[head, item, way], near_recv.at[head, item, way], sides[way])

    def far_copy(head, item, pair):
        view = kv.at[head, pair, 0, rows_of(item)]
        return remote(view, view, far_send.at[head, item], far_recv.at[head, item], right_at)

    def upper_copy(head, source, target):
        view = kv.at[head, source, 1, own_rows]
        return remote(
            view, view, up_send.at[head, target], up_recv.at[head, source], at_member(target * 2 + odd)
        )

    def turned_copy(head, pair, item):
        view = kv.at[head, pair, 1, rows_of(item)]
        return remote(view, view, turn_send.at[head, pair], turn_recv.at[head, pair], partner_at)

    def gather_0(head):
        partner_copy(head).start()
        near_copy(head, 0, 0, half_me).start()
        near_copy(head, 0, 1, half_me).start()
        for target in (0, 1, 2):
            when(target < half_me, lambda: upper_copy(head, half_me, target).start())
        turned_copy(head, half_me, 0).start()

    def gather_1(head):
        partner_copy(head).wait_recv()
        near_copy(head, 1, 0, half_me).start()
        near_copy(head, 1, 1, half_me).start()

    def gather_2(head):
        near_copy(head, 0, 1, left).wait_recv()
        far_copy(head, 0, left).start()
        near_copy(head, 0, 0, right).wait_recv()

    def gather_3(head):
        def turn_on(pair):
            upper_copy(head, pair, half_me).wait_recv()
            turned_copy(head, pair, 0).start()

        for pair in (1, 2, 3):
            when(pair > half_me, turn_on, pair)
        near_copy(head, 1, 1, left).wait_recv()
        far_copy(head, 1, left).start()
        near_copy(head, 1, 0, right).wait_recv()

    def gather_4(head):
        for pair in range(4):
            when(pair >= half_me, lambda: turned_copy(head, pair, 1).wait_recv())
        far_copy(head, 0, across).wait_recv()
        far_copy(head, 1, across).wait_recv()

    def gather_end(head):
        partner_copy(head).wait_send()
        for item in range(2):
            near_copy(head, item, 0, half_me).wait_send()
            near_copy(head, item, 1, half_me).wait_send()
            far_copy(head, item, left).wait_send()
        for target in (0, 1, 2):
            when(target < half_me, lambda: upper_copy(head, half_me, target).wait_send())
        for pair in range(4):
            when(pair >= half_me, lambda: turned_copy(head, pair, 0).wait_send())

    gather_0(0)
    send_weights(sum_block, me, SPAN_MAX, 0, lambda step: at_member(peer_of(step)))

    span = span_ref[0, cp]
    spread = span > 1
    row_id = lax.broadcasted_iota(jnp.int32, (HALF, HALF), 0)
    col_id = lax.broadcasted_iota(jnp.int32, (HALF, HALF), 1)
    slot_of = {}
    for name, ids in (("q0", row_id), ("q1", row_id + HALF), ("k0", col_id), ("k1", col_id + HALF)):
        slot_count = jnp.zeros((HALF, HALF), jnp.int32)
        end = jnp.int32(0)
        for slot in range(SLOTS):
            end = end + len_ref[0, slot, cp]
            slot_count = slot_count + (ids >= end).astype(jnp.int32)
        slot_of[name] = slot_count
    spread_add = jnp.where(spread, 1, 0)

    def same_document(q_name, k_name):
        equal = (slot_of[q_name] == slot_of[k_name]).astype(jnp.int32) + spread_add
        return jnp.where(equal > 0, 0.0, NEG)

    causal = jnp.where(col_id <= row_id, 0.0, NEG)
    own_lower = jnp.minimum(same_document("q0", "k0"), causal)
    own_upper = jnp.minimum(same_document("q1", "k1"), causal)
    own_cross = same_document("q1", "k0")

    partner_seen = jnp.where(span > 1, 0.0, NEG)
    for side in range(2):
        lanes = slice(side * HALF, (side + 1) * HALF)
        is_me = jnp.where(odd == side, 1, 0) + jnp.zeros((HALF, HALF), jnp.int32) > 0
        after = jnp.where(odd > side, 0.0, NEG)
        before = jnp.where(odd < side, 0.0, NEG)
        bias[0, :, lanes] = jnp.where(is_me, own_cross, partner_seen)
        bias[1, :, lanes] = jnp.where(is_me, own_lower, jnp.minimum(partner_seen, after))
        bias[2, :, lanes] = jnp.where(is_me, own_upper, jnp.minimum(partner_seen, before))
    seen = {}
    for visit, pair_step in ((0, 2), (2, 3), (4, 1)):
        other = lax.rem(half_me + pair_step, 4) * 2
        seen[visit] = seen[visit + 1] = jnp.where(lax.bitwise_xor(other, me) < span, 0.0, NEG)

    gather_1(0)

    for head in range(KV_HEADS):
        load_queries(head).wait()

    def turn_queries(index, carry):
        for head in range(2):
            lanes = pl.ds(pl.multiple_of((index * 2 + head) * HEAD_DIM, HEAD_DIM), HEAD_DIM)
            for half in range(2):
                part = q_ref[half * HALF : (half + 1) * HALF, lanes]
                q_t[index, half, :, head * HALF : (head + 1) * HALF] = part.T
        return carry

    lax.fori_loop(0, HEADS // 2, turn_queries, 0)

    gather_2(0)
    gather_0(1)
    for head in range(KV_HEADS):
        load_grads(head).wait()
    for half in range(2):
        rows = slice(half * HALF, (half + 1) * HALF)
        scaled = jnp.broadcast_to(w_ref[0:1, rows], (HALF, HALF)).T

        def weigh(index, carry, rows=rows, half=half, scaled=scaled):
            for head in range(2):
                lanes = pl.ds(pl.multiple_of((index * 2 + head) * HEAD_DIM, HEAD_DIM), HEAD_DIM)
                part = (g_ref[rows, lanes].astype(F32) * scaled).astype(BF16)
                dout[rows, lanes] = part
                d_t[index, half, :, head * HALF : (head + 1) * HALF] = part.T
            return carry

        lax.fori_loop(0, HEADS // 2, weigh, 0)
    gather_3(0)
    gather_1(1)

    def weights_1():
        sum_dp[dp] = wait_weights(sum_block, me, SPAN_MAX, 0, lambda step: at_member(peer_of(step)))
        send_weights(sum_dp, dp, n_dp, 8, at_dp)

    def weights_2():
        sum_y[block] = wait_weights(sum_dp, dp, n_dp, 8, at_dp)
        send_weights(sum_y, block, n_blocks, 16, at_block)

    def weights_3():
        rows_total = ROWS_DEV * SPAN_MAX * n_dp * n_blocks
        inverse_mean[...] = rows_total / wait_weights(sum_y, block, n_blocks, 16, at_block)

    pairs = (across, across, left, left, right, right, half_me, half_me, half_me)

    def half_of(visit):
        if visit in (1, 3, 5):
            return jnp.where(pairs[visit] < half_me, 0, 1)
        return 0 if visit == 7 else 1

    def key_half(visit):
        if visit in (1, 3, 5):
            return jnp.where(pairs[visit] < half_me, 0, 1)
        return 1 if visit == 8 else 0

    def lanes_of(index, part):
        return pl.ds(pl.multiple_of((index * 2 + part) * HEAD_DIM, HEAD_DIM), HEAD_DIM)

    def rows_at(half):
        if isinstance(half, int):
            return pl.ds(half * HALF, HALF)
        return pl.ds(pl.multiple_of(half * HALF, HALF), HALF)

    def keys_of(head, visit):
        return kv[head, pairs[visit], key_half(visit), :, 0:HEAD_DIM]

    def values_of(head, visit):
        return kv[head, pairs[visit], key_half(visit), :, HEAD_DIM : 2 * HEAD_DIM]

    def fold(op, block):
        return op(block[:, :HALF], block[:, HALF:])

    def wide(block):
        return jnp.concatenate([block, block], axis=1)

    def score_steps(head, tile):
        index = head * TILES + tile
        slot = tile % 2
        tops = {}

        def start():
            row_max[slot] = jnp.full(row_max.shape[1:], NEG, F32)

        def score(visit):
            half = half_of(visit)
            keys = keys_of(head, visit)
            for part in range(2):
                scores = dot_nt(q_ref[rows_at(half), lanes_of(index, part)], keys)
                if visit >= 6:
                    scores = scores + bias[visit - 6]
                s_scr[slot, visit, part] = scores
                folded = fold(jnp.maximum, scores)
                if visit < 6:
                    folded = folded + seen[visit]
                if isinstance(half, int):
                    known = tops.get((half, part))
                    tops[half, part] = folded if known is None else jnp.maximum(known, folded)
                else:
                    row_max[slot, half, part] = jnp.maximum(row_max[slot, half, part], folded)

        def end():
            for half in range(2):
                for part in range(2):
                    top = jnp.maximum(row_max[slot, half, part], tops[half, part])
                    row_max[slot, half, part] = jnp.broadcast_to(
                        jnp.max(top, axis=1, keepdims=True), (HALF, HALF)
                    )

        return start, score, end

    def attend_steps(head, tile):
        index = head * TILES + tile
        slot = tile % 2
        kept = {}
        ones = jnp.ones((PAIR, HALF), BF16)

        def start():
            o_fold[...] = jnp.zeros(o_fold.shape, F32)

        def attend(visit):
            half = half_of(visit)
            values = jnp.concatenate([values_of(head, visit), ones], axis=1)
            for part in range(2):
                top = row_max[slot, half, part]
                if visit < 6:
                    top = top - seen[visit]
                probs = jnp.exp2((s_scr[slot, visit, part] - wide(top)) * SCALE_LOG2).astype(BF16)
                p_scr[visit, tile, part * HALF : (part + 1) * HALF, :] = probs
                if isinstance(half, int):
                    kept.setdefault((half, part), []).append((probs, values))
                else:
                    o_fold[half, part] = o_fold[half, part] + dot(probs, values)

        def end():
            for half in range(2):
                rows = slice(half * HALF, (half + 1) * HALF)
                for part in range(2):
                    probs = jnp.concatenate([pair[0] for pair in kept[half, part]], axis=1)
                    values = jnp.concatenate([pair[1] for pair in kept[half, part]], axis=0)
                    both = dot(probs, values) + o_fold[half, part]
                    inverse = 1.0 / both[:, HEAD_DIM:]
                    place = slice(tile * PAIR + part * HALF, tile * PAIR + (part + 1) * HALF)
                    inverses[half, place, :] = inverse
                    out = (both[:, :HEAD_DIM] * inverse).astype(BF16)
                    o_ref[rows, lanes_of(index, part)] = out
                    product = dout[rows, lanes_of(index, part)].astype(F32) * out.astype(F32)
                    delta[half, place, :] = jnp.broadcast_to(
                        jnp.sum(product, axis=1, keepdims=True), (HALF, HALF)
                    )
                    turned = inverse.T
                    lanes = slice(part * HALF, (part + 1) * HALF)
                    qt_scaled[half, tile, :, lanes] = (q_t[index, half, :, lanes].astype(F32) * turned).astype(BF16)
                    dt_scaled[half, tile, :, lanes] = (d_t[index, half, :, lanes].astype(F32) * turned).astype(BF16)

        return start, attend, end

    def forward_step(head, score_tile, attend_tile):
        running = []
        if score_tile is not None:
            running.append(score_steps(head, score_tile))
        if attend_tile is not None:
            running.append(attend_steps(head, attend_tile))
        for steps in running:
            steps[0]()
        for visit in FORWARD_ORDER:
            for steps in running:
                steps[1](visit)
        for steps in running:
            steps[2]()

    def backward_visits(head, visits):
        steps = [(visit, tile) for visit in visits for tile in range(TILES)]
        dprobs = {}

        def begin(step):
            visit, tile = step
            index = head * TILES + tile
            values = values_of(head, visit)
            rows = rows_at(half_of(visit))
            dprobs[step] = [dot_nt(dout[rows, lanes_of(index, part)], values) for part in range(2)]

        begin(steps[0])
        parity = lax.rem(head, 2)
        for number, step in enumerate(steps):
            if number + 1 < len(steps):
                begin(steps[number + 1])
            visit, tile = step
            half = half_of(visit)
            keys = keys_of(head, visit)
            halves = []
            for part in range(2):
                place = slice(tile * PAIR + part * HALF, tile * PAIR + (part + 1) * HALF)
                probs = p_scr[visit, tile, part * HALF : (part + 1) * HALF, :]
                dscore = probs.astype(F32) * (dprobs[step][part] - wide(delta[half, place, :]))
                dscore = dscore.astype(BF16)
                halves.append(dscore)
                dq_acc[half, place, :] = dq_acc[half, place, :] + dot(dscore, keys)
            dk_part = dot(qt_scaled[half, tile], jnp.concatenate(halves, axis=0))
            dv_part = dot(dt_scaled[half, tile], p_scr[visit, tile])
            dkey = dk_part if tile == 0 else dkey + dk_part
            dvalue = dv_part if tile == 0 else dvalue + dv_part
            if tile == TILES - 1:
                pair, side = pairs[visit], key_half(visit)
                acc[parity, pair, side, 0:HEAD_DIM] = acc[parity, pair, side, 0:HEAD_DIM] + dkey
                acc[parity, pair, side, HEAD_DIM : 2 * HEAD_DIM] = (
                    acc[parity, pair, side, HEAD_DIM : 2 * HEAD_DIM] + dvalue
                )

    def close_head(head):
        for tile in range(TILES):
            index = head * TILES + tile
            tile_rows = slice(tile * PAIR, (tile + 1) * PAIR)
            for half in range(2):
                result = (
                    dq_acc[half, tile_rows, :] * (inverses[half, tile_rows, :] * (inverse_mean[0:1, :] * SCALE))
                ).astype(BF16)
                rows = slice(half * HALF, (half + 1) * HALF)
                dq_ref[rows, lanes_of(index, 0)] = result[:HALF]
                dq_ref[rows, lanes_of(index, 1)] = result[HALF:]

    def first_copy(head):
        return remote(first_out.at[head], first_in.at[head], first_send.at[head], first_recv.at[head], left_at)

    def second_copy(head, way):
        return remote(
            second_out.at[head, way],
            second_in.at[head, way],
            second_send.at[head, way],
            second_recv.at[head, way],
            sides[way],
        )

    def last_copy(head):
        return remote(last_out.at[head], last_in.at[head], last_send.at[head], last_recv.at[head], partner_at)

    def cross_copy(head, pair):
        return remote(
            cross_out.at[head, pair],
            cross_in.at[head, pair],
            cross_send.at[head, pair],
            cross_recv.at[head, pair],
            partner_at,
        )

    def owed_copy(head, source, target):
        return remote(
            owed_out.at[head, target],
            owed_in.at[head, source],
            owed_send.at[head, target],
            owed_recv.at[head, source],
            at_member(target * 2 + odd),
        )

    def cross_start(head, pair):
        cross_out[head, pair] = acc[lax.rem(head, 2), pair, 1, :, other_rows].astype(BF16)
        cross_copy(head, pair).start()

    def scatter_1(head):
        first_out[head] = acc[lax.rem(head, 2), across, 0].astype(BF16)
        first_copy(head).start()
        when(half_me < 2, cross_start, head, across)

    def scatter_2(head):
        second_out[head, 1] = acc[lax.rem(head, 2), right, 0].astype(BF16)
        second_copy(head, 1).start()
        when(half_me < 3, cross_start, head, right)
        when(half_me == 0, cross_start, head, left)

    def scatter_3(head):
        cross_start(head, half_me)
        first_copy(head).wait_recv()
        second_out[head, 0] = (acc[lax.rem(head, 2), left, 0] + first_in[head].astype(F32)).astype(BF16)
        second_copy(head, 0).start()

    def scatter_4(head):
        def pay(pair):
            cross_copy(head, pair).wait_recv()
            total = acc[lax.rem(head, 2), pair, 1, :, own_rows] + cross_in[head, pair].astype(F32)
            owed_out[head, pair] = total.astype(BF16)
            owed_copy(head, half_me, pair).start()

        for pair in (1, 2, 3):
            when(pair > half_me, pay, pair)

    def scatter_5(head):
        parity = lax.rem(head, 2)
        second_copy(head, 0).wait_recv()
        second_copy(head, 1).wait_recv()
        acc[parity, half_me, 0] = acc[parity, half_me, 0] + (
            second_in[head, 0].astype(F32) + second_in[head, 1].astype(F32)
        )
        last_out[head] = acc[parity, half_me, 0, :, other_rows].astype(BF16)
        last_copy(head).start()

    def scatter_6(head):
        parity = lax.rem(head, 2)
        lanes = pl.ds(pl.multiple_of(head * HEAD_DIM, HEAD_DIM), HEAD_DIM)

        def settle(side, total):
            rows = slice(side * HALF, (side + 1) * HALF)
            scale = inverse_mean[0:1, :]
            dk_ref[rows, lanes] = (total[:HEAD_DIM] * (scale * SCALE)).T.astype(BF16)
            dv_ref[rows, lanes] = (total[HEAD_DIM:] * scale).T.astype(BF16)

        def collect(source):
            owed_copy(head, source, half_me).wait_recv()
            acc[parity, half_me, 1, :, own_rows] = acc[parity, half_me, 1, :, own_rows] + owed_in[
                head, source
            ].astype(F32)

        for source in (0, 1, 2):
            when(source < half_me, collect, source)
        cross_copy(head, half_me).wait_recv()
        settle(1, acc[parity, half_me, 1, :, own_rows] + cross_in[head, half_me].astype(F32))
        last_copy(head).wait_recv()
        settle(0, acc[parity, half_me, 0, :, own_rows] + last_in[head].astype(F32))

    def scatter_end(head):
        first_copy(head).wait_send()
        second_copy(head, 0).wait_send()
        second_copy(head, 1).wait_send()
        last_copy(head).wait_send()
        for pair in range(4):
            when(pair >= half_me, lambda: cross_copy(head, pair).wait_send())
        for pair in (1, 2, 3):
            when(pair > half_me, lambda: owed_copy(head, half_me, pair).wait_send())

    def head_step(head, carry):
        gather_4(head)
        acc[lax.rem(head, 2)] = jnp.zeros(acc.shape[1:], F32)
        dq_acc[...] = jnp.zeros(dq_acc.shape, F32)
        more = head < KV_HEADS - 1
        earlier = head > 0

        first = head == 0

        forward_step(head, 0, None)
        when(more, gather_2, head + 1)
        when(first, weights_1)
        forward_step(head, 1, 0)
        when(first, weights_2)
        when(earlier, scatter_4, head - 1)
        forward_step(head, 2, 1)
        when(more, gather_3, head + 1)
        when(first, weights_3)
        forward_step(head, 3, 2)
        forward_step(head, None, 3)
        save_out(head).start()
        when(head < KV_HEADS - 2, gather_0, head + 2)
        backward_visits(head, (0, 1))
        scatter_1(head)
        when(earlier, scatter_5, head - 1)
        backward_visits(head, (2, 3, 4, 5))
        scatter_2(head)
        when(head < KV_HEADS - 2, gather_1, head + 2)
        backward_visits(head, (6, 7, 8))
        scatter_3(head)
        close_head(head)
        save_dquery(head).start()
        when(earlier, scatter_6, head - 1)
        return carry

    lax.fori_loop(0, KV_HEADS, head_step, 0)
    scatter_4(KV_HEADS - 1)
    scatter_5(KV_HEADS - 1)
    scatter_6(KV_HEADS - 1)

    def finish(head, carry):
        gather_end(head)
        scatter_end(head)
        save_out(head).wait()
        save_dquery(head).wait()
        return carry

    lax.fori_loop(0, KV_HEADS, finish, 0)


CHUNKS = 4


def carry_kernel(count, *refs):
    sources, targets, slots = refs[:count], refs[count : 2 * count], refs[2 * count : 3 * count]
    sem = refs[3 * count]

    def copies(number, chunk):
        rows = sources[number].shape[0] // CHUNKS
        place = pl.ds(chunk * rows, rows)
        arrive = pltpu.make_async_copy(
            sources[number].at[place], slots[number].at[place], sem.at[0, number, chunk]
        )
        leave = pltpu.make_async_copy(
            slots[number].at[place], targets[number].at[place], sem.at[1, number, chunk]
        )
        return arrive, leave

    steps = [copies(number, chunk) for chunk in range(CHUNKS) for number in range(count)]
    for arrive, _ in steps:
        arrive.start()
    for arrive, leave in steps:
        arrive.wait()
        leave.start()
    for _, leave in steps:
        leave.wait()


def carry_out(*arrays):
    hbm = pl.BlockSpec(memory_space=pl.ANY)
    count = len(arrays)
    return pl.pallas_call(
        functools.partial(carry_kernel, count),
        out_shape=tuple(jax.ShapeDtypeStruct(array.shape, array.dtype) for array in arrays),
        in_specs=[hbm] * count,
        out_specs=(hbm,) * count,
        scratch_shapes=[pltpu.VMEM(array.shape, array.dtype) for array in arrays]
        + [pltpu.SemaphoreType.DMA((2, count, CHUNKS))],
        compiler_params=pltpu.CompilerParams(vmem_limit_bytes=56 * 1024 * 1024),
    )(*arrays)


def on_device(n_dp, n_blocks, queries, key_states, value_states, grad_out, token_weight, span_size, short_lengths):
    vmem = pl.BlockSpec(memory_space=pltpu.VMEM)
    smem = pl.BlockSpec(memory_space=pltpu.SMEM)
    hbm = pl.BlockSpec(memory_space=pl.ANY)
    wide = jax.ShapeDtypeStruct((ROWS_DEV, HEADS * HEAD_DIM), BF16)
    narrow = jax.ShapeDtypeStruct((ROWS_DEV, KV_HEADS * HEAD_DIM), BF16)
    all_rows = (2, TILES * PAIR, HEAD_DIM)
    results = pl.pallas_call(
        functools.partial(kernel, n_dp, n_blocks),
        out_shape=(wide, wide, narrow, narrow),
        in_specs=[hbm, vmem, vmem, hbm, vmem, smem, smem],
        out_specs=(hbm, hbm, vmem, vmem),
        scratch_shapes=[
            pltpu.VMEM((ROWS_DEV, HEADS * HEAD_DIM), BF16),
            pltpu.VMEM((ROWS_DEV, HEADS * HEAD_DIM), BF16),
            pltpu.VMEM((ROWS_DEV, HEADS * HEAD_DIM), BF16),
            pltpu.VMEM((ROWS_DEV, HEADS * HEAD_DIM), BF16),
            pltpu.VMEM((KV_HEADS, 4, 2, PAIR, 2 * HEAD_DIM), BF16),
            pltpu.VMEM((KV_HEADS, 2 * HEAD_DIM, PAIR), BF16),
            pltpu.VMEM((KV_HEADS, 2 * HEAD_DIM, PAIR), BF16),
            pltpu.VMEM((KV_HEADS, 2, 2 * HEAD_DIM, PAIR), BF16),
            pltpu.VMEM((KV_HEADS, 2, 2 * HEAD_DIM, PAIR), BF16),
            pltpu.VMEM((KV_HEADS, 2 * HEAD_DIM, HALF), BF16),
            pltpu.VMEM((KV_HEADS, 2 * HEAD_DIM, HALF), BF16),
            pltpu.VMEM((KV_HEADS, 4, 2 * HEAD_DIM, HALF), BF16),
            pltpu.VMEM((KV_HEADS, 4, 2 * HEAD_DIM, HALF), BF16),
            pltpu.VMEM((KV_HEADS, 4, 2 * HEAD_DIM, HALF), BF16),
            pltpu.VMEM((KV_HEADS, 4, 2 * HEAD_DIM, HALF), BF16),
            pltpu.VMEM((HEADS // 2, 2, HEAD_DIM, PAIR), BF16),
            pltpu.VMEM((HEADS // 2, 2, HEAD_DIM, PAIR), BF16),
            pltpu.VMEM((ROWS_DEV, HEADS * HEAD_DIM), BF16),
            pltpu.VMEM((3, HALF, PAIR), F32),
            pltpu.VMEM((2, VISITS, 2, HALF, PAIR), F32),
            pltpu.VMEM((VISITS, TILES, PAIR, PAIR), BF16),
            pltpu.VMEM((2, 4, 2, 2 * HEAD_DIM, PAIR), F32),
            pltpu.VMEM((2, 2, 2, HALF, HALF), F32),
            pltpu.VMEM((2, 2, HALF, PAIR), F32),
            pltpu.VMEM(all_rows, F32),
            pltpu.VMEM(all_rows, F32),
            pltpu.VMEM(all_rows, F32),
            pltpu.VMEM((2, TILES, HEAD_DIM, PAIR), BF16),
            pltpu.VMEM((2, TILES, HEAD_DIM, PAIR), BF16),
            pltpu.VMEM((SPAN_MAX, 8, 128), F32),
            pltpu.VMEM((n_dp, 8, 128), F32),
            pltpu.VMEM((n_blocks, 8, 128), F32),
            pltpu.VMEM((8, 128), F32),
            pltpu.SemaphoreType.DMA((2, KV_HEADS)),
            pltpu.SemaphoreType.DMA((2, KV_HEADS)),
            pltpu.SemaphoreType.DMA((KV_HEADS,)),
            pltpu.SemaphoreType.DMA((KV_HEADS,)),
            pltpu.SemaphoreType.DMA((KV_HEADS, 2, 2)),
            pltpu.SemaphoreType.DMA((KV_HEADS, 2, 2)),
            pltpu.SemaphoreType.DMA((KV_HEADS, 2)),
            pltpu.SemaphoreType.DMA((KV_HEADS, 2)),
            pltpu.SemaphoreType.DMA((KV_HEADS, 4)),
            pltpu.SemaphoreType.DMA((KV_HEADS, 4)),
            pltpu.SemaphoreType.DMA((KV_HEADS, 4)),
            pltpu.SemaphoreType.DMA((KV_HEADS, 4)),
            pltpu.SemaphoreType.DMA((KV_HEADS,)),
            pltpu.SemaphoreType.DMA((KV_HEADS,)),
            pltpu.SemaphoreType.DMA((KV_HEADS, 2)),
            pltpu.SemaphoreType.DMA((KV_HEADS, 2)),
            pltpu.SemaphoreType.DMA((KV_HEADS,)),
            pltpu.SemaphoreType.DMA((KV_HEADS,)),
            pltpu.SemaphoreType.DMA((KV_HEADS, 4)),
            pltpu.SemaphoreType.DMA((KV_HEADS, 4)),
            pltpu.SemaphoreType.DMA((KV_HEADS, 4)),
            pltpu.SemaphoreType.DMA((KV_HEADS, 4)),
            pltpu.SemaphoreType.DMA((24,)),
            pltpu.SemaphoreType.DMA((24,)),
        ],
        compiler_params=pltpu.CompilerParams(
            collective_id=0, has_side_effects=True, vmem_limit_bytes=56 * 1024 * 1024
        ),
    )(
        queries,
        key_states,
        value_states,
        grad_out,
        token_weight.reshape(1, ROWS_DEV),
        span_size,
        jnp.swapaxes(short_lengths, 1, 2),
    )
    return carry_out(*results)


def solution(mesh):
    rows = P(("dp", "cp"), None)
    n_dp = mesh.shape["dp"]
    n_blocks = mesh.shape["cp"] // SPAN_MAX
    return jax.shard_map(
        functools.partial(on_device, n_dp, n_blocks),
        mesh=mesh,
        in_specs=(rows, rows, rows, rows, P(("dp", "cp")), P("dp", None), P("dp", None, None)),
        out_specs=(rows, rows, rows, rows),
        check_vma=False,
    )
```

time: 150 us -> 98.2 us (0.65)
  the two profiles are of different devices: /device:TPU:0 before, /device:TPU:20 now
where the time goes in v2:
time: 98.2 us; the launch traced here: 98 us
  Pallas kernels  97.4 us (99%)
    pallas_call x1, Pallas kernels, on_device(): pl.pallas_call(functools.partial(kernel, n_dp, n_blocks), out_shape=(wide...  93.2 us
    pallas_call x1, Pallas kernels, carry_out(): pl.pallas_call(functools.partial(carry_kernel, count), out_shape=tuple((j...  4.18 us

profile of v2, /device:TPU:20, one launch (start us, length us, event | category | flops | bytes accessed | tf_op | source)
XLA Modules:
  0.0 98.0 jit_solution(8960708737072037268)
XLA Ops:
  0.6 93.2 %shard_map.102 = (bf16[256,4096]{1,0:T(8,128)(2,1)}, bf16[256,4096]{1,0:T(8,128)(2,1)}, bf16[256,512]{1,0:T(8,128)(2,1)}, bf16[256,512]{1,0:T(8,128)(2,1)}) custom-call(bf16[256,4096]{1,0:T(8,128)(2,1)} %q_hbm.1, bf16[256,512]{1,0:T(8,128)(2,1)} %k_ref.1, bf16[256,512]{1,0:T(8,128)(2,1)} %v_ref.1, bf16[256,4096]{1,0:T(8,128)(2,1)} %g_hbm.1, ...), custom_call_target="tpu_custom_call" | custom-call | tf_op jit(solution)/shard_map/pallas_call | solution.py:767
  93.8 4.2 %shard_map.103 = (bf16[256,4096]{1,0:T(8,128)(2,1)}, bf16[256,4096]{1,0:T(8,128)(2,1)}, bf16[256,512]{1,0:T(8,128)(2,1)}, bf16[256,512]{1,0:T(8,128)(2,1)}) custom-call(bf16[256,4096]{1,0:T(8,128)(2,1)} %get-tuple-element.8.refs_0_, bf16[256,4096]{1,0:T(8,128)(2,1)} %get-tuple-element.9.refs_1_, bf16[256,512]{1,0:T(8,128)(2,1)} %get-tuple-element.10.refs_2_, ...), custom_call_target="tpu_custom_call" | custom-call | tf_op jit(solution)/shard_map/pallas_call | solution.py:749

commit v3 on v2

--- a/solution.py
+++ b/solution.py
@@ -236,7 +236,7 @@
 
     def far_copy(head, item, pair):
         view = kv.at[head, pair, 0, rows_of(item)]
-        return remote(view, view, far_send.at[head, item], far_recv.at[head, item], right_at)
+        return remote(view, view, far_send.at[head, item], far_recv.at[head, item], sides[1 - item])
 
     def upper_copy(head, source, target):
         view = kv.at[head, source, 1, own_rows]
@@ -266,16 +266,22 @@
         far_copy(head, 0, left).start()
         near_copy(head, 0, 0, right).wait_recv()
 
-    def gather_3(head):
+    def gather_turn(head):
         def turn_on(pair):
             upper_copy(head, pair, half_me).wait_recv()
             turned_copy(head, pair, 0).start()
 
         for pair in (1, 2, 3):
             when(pair > half_me, turn_on, pair)
+
+    def gather_forward(head):
+        near_copy(head, 1, 0, right).wait_recv()
+        far_copy(head, 1, right).start()
         near_copy(head, 1, 1, left).wait_recv()
-        far_copy(head, 1, left).start()
-        near_copy(head, 1, 0, right).wait_recv()
+
+    def gather_3(head):
+        gather_turn(head)
+        gather_forward(head)
 
     def gather_4(head):
         for pair in range(4):
@@ -288,7 +294,7 @@
         for item in range(2):
             near_copy(head, item, 0, half_me).wait_send()
             near_copy(head, item, 1, half_me).wait_send()
-            far_copy(head, item, left).wait_send()
+            far_copy(head, item, (left, right)[item]).wait_send()
         for target in (0, 1, 2):
             when(target < half_me, lambda: upper_copy(head, half_me, target).wait_send())
         for pair in range(4):
@@ -335,39 +341,32 @@
         seen[visit] = seen[visit + 1] = jnp.where(lax.bitwise_xor(other, me) < span, 0.0, NEG)
 
     gather_1(0)
-
-    for head in range(KV_HEADS):
-        load_queries(head).wait()
-
-    def turn_queries(index, carry):
-        for head in range(2):
-            lanes = pl.ds(pl.multiple_of((index * 2 + head) * HEAD_DIM, HEAD_DIM), HEAD_DIM)
-            for half in range(2):
-                part = q_ref[half * HALF : (half + 1) * HALF, lanes]
-                q_t[index, half, :, head * HALF : (head + 1) * HALF] = part.T
-        return carry
-
-    lax.fori_loop(0, HEADS // 2, turn_queries, 0)
-
+    gather_turn(0)
     gather_2(0)
     gather_0(1)
-    for head in range(KV_HEADS):
+    gather_forward(0)
+
+    def prepare(head):
+        load_queries(head).wait()
         load_grads(head).wait()
-    for half in range(2):
-        rows = slice(half * HALF, (half + 1) * HALF)
-        scaled = jnp.broadcast_to(w_ref[0:1, rows], (HALF, HALF)).T
-
-        def weigh(index, carry, rows=rows, half=half, scaled=scaled):
-            for head in range(2):
-                lanes = pl.ds(pl.multiple_of((index * 2 + head) * HEAD_DIM, HEAD_DIM), HEAD_DIM)
-                part = (g_ref[rows, lanes].astype(F32) * scaled).astype(BF16)
-                dout[rows, lanes] = part
-                d_t[index, half, :, head * HALF : (head + 1) * HALF] = part.T
+        scaled = [jnp.broadcast_to(w_ref[0:1, half * HALF : (half + 1) * HALF], (HALF, HALF)).T for half in range(2)]
+
+        def turn(tile, carry):
+            index = head * TILES + tile
+            for part in range(2):
+                lanes = pl.ds(pl.multiple_of((index * 2 + part) * HEAD_DIM, HEAD_DIM), HEAD_DIM)
+                columns = slice(part * HALF, (part + 1) * HALF)
+                for half in range(2):
+                    rows = slice(half * HALF, (half + 1) * HALF)
+                    q_t[index, half, :, columns] = q_ref[rows, lanes].T
+                    weighted = (g_ref[rows, lanes].astype(F32) * scaled[half]).astype(BF16)
+                    dout[rows, lanes] = weighted
+                    d_t[index, half, :, columns] = weighted.T
             return carry
 
-        lax.fori_loop(0, HEADS // 2, weigh, 0)
-    gather_3(0)
-    gather_1(1)
+        lax.fori_loop(0, TILES, turn, 0)
+
+    prepare(0)
 
     def weights_1():
         sum_dp[dp] = wait_weights(sum_block, me, SPAN_MAX, 0, lambda step: at_member(peer_of(step)))
@@ -520,7 +519,7 @@
             dprobs[step] = [dot_nt(dout[rows, lanes_of(index, part)], values) for part in range(2)]
 
         begin(steps[0])
-        parity = lax.rem(head, 2)
+        parity = lax.rem(head, 3)
         for number, step in enumerate(steps):
             if number + 1 < len(steps):
                 begin(steps[number + 1])
@@ -558,8 +557,14 @@
                 dq_ref[rows, lanes_of(index, 0)] = result[:HALF]
                 dq_ref[rows, lanes_of(index, 1)] = result[HALF:]
 
-    def first_copy(head):
-        return remote(first_out.at[head], first_in.at[head], first_send.at[head], first_recv.at[head], left_at)
+    def first_copy(head, way):
+        return remote(
+            first_out.at[head, way],
+            first_in.at[head, way],
+            first_send.at[head, way],
+            first_recv.at[head, way],
+            sides[way],
+        )
 
     def second_copy(head, way):
         return remote(
@@ -592,30 +597,32 @@
         )
 
     def cross_start(head, pair):
-        cross_out[head, pair] = acc[lax.rem(head, 2), pair, 1, :, other_rows].astype(BF16)
+        cross_out[head, pair] = acc[lax.rem(head, 3), pair, 1, :, other_rows].astype(BF16)
         cross_copy(head, pair).start()
 
     def scatter_1(head):
-        first_out[head] = acc[lax.rem(head, 2), across, 0].astype(BF16)
-        first_copy(head).start()
+        for way in range(2):
+            first_out[head, way] = acc[lax.rem(head, 3), across, 0, :, rows_of(way)].astype(BF16)
+            first_copy(head, way).start()
         when(half_me < 2, cross_start, head, across)
 
     def scatter_2(head):
-        second_out[head, 1] = acc[lax.rem(head, 2), right, 0].astype(BF16)
-        second_copy(head, 1).start()
         when(half_me < 3, cross_start, head, right)
         when(half_me == 0, cross_start, head, left)
 
     def scatter_3(head):
-        cross_start(head, half_me)
-        first_copy(head).wait_recv()
-        second_out[head, 0] = (acc[lax.rem(head, 2), left, 0] + first_in[head].astype(F32)).astype(BF16)
-        second_copy(head, 0).start()
+        parity = lax.rem(head, 3)
+        for way, pair in ((0, left), (1, right)):
+            first_copy(head, way).wait_recv()
+            mixed = acc[parity, pair, 0, :, rows_of(way)] + first_in[head, way].astype(F32)
+            second_out[head, way, :, rows_of(way)] = mixed.astype(BF16)
+            second_out[head, way, :, rows_of(1 - way)] = acc[parity, pair, 0, :, rows_of(1 - way)].astype(BF16)
+            second_copy(head, way).start()
 
     def scatter_4(head):
         def pay(pair):
             cross_copy(head, pair).wait_recv()
-            total = acc[lax.rem(head, 2), pair, 1, :, own_rows] + cross_in[head, pair].astype(F32)
+            total = acc[lax.rem(head, 3), pair, 1, :, own_rows] + cross_in[head, pair].astype(F32)
             owed_out[head, pair] = total.astype(BF16)
             owed_copy(head, half_me, pair).start()
 
@@ -623,7 +630,7 @@
             when(pair > half_me, pay, pair)
 
     def scatter_5(head):
-        parity = lax.rem(head, 2)
+        parity = lax.rem(head, 3)
         second_copy(head, 0).wait_recv()
         second_copy(head, 1).wait_recv()
         acc[parity, half_me, 0] = acc[parity, half_me, 0] + (
@@ -633,7 +640,7 @@
         last_copy(head).start()
 
     def scatter_6(head):
-        parity = lax.rem(head, 2)
+        parity = lax.rem(head, 3)
         lanes = pl.ds(pl.multiple_of(head * HEAD_DIM, HEAD_DIM), HEAD_DIM)
 
         def settle(side, total):
@@ -656,7 +663,8 @@
         settle(0, acc[parity, half_me, 0, :, own_rows] + last_in[head].astype(F32))
 
     def scatter_end(head):
-        first_copy(head).wait_send()
+        first_copy(head, 0).wait_send()
+        first_copy(head, 1).wait_send()
         second_copy(head, 0).wait_send()
         second_copy(head, 1).wait_send()
         last_copy(head).wait_send()
@@ -667,41 +675,52 @@
 
     def head_step(head, carry):
         gather_4(head)
-        acc[lax.rem(head, 2)] = jnp.zeros(acc.shape[1:], F32)
+        acc[lax.rem(head, 3)] = jnp.zeros(acc.shape[1:], F32)
         dq_acc[...] = jnp.zeros(dq_acc.shape, F32)
-        more = head < KV_HEADS - 1
         earlier = head > 0
 
         first = head == 0
 
+        second = head == 1
+        third = head == 2
         forward_step(head, 0, None)
-        when(more, gather_2, head + 1)
+        when(first, gather_1, 1)
+        when(third, gather_3, 3)
         when(first, weights_1)
         forward_step(head, 1, 0)
+        when(first, gather_0, 2)
+        when(second, gather_3, 2)
         when(first, weights_2)
-        when(earlier, scatter_4, head - 1)
         forward_step(head, 2, 1)
-        when(more, gather_3, head + 1)
+        when(first, gather_2, 1)
+        when(second, gather_1, 3)
+        when(head > 1, scatter_6, head - 2)
         when(first, weights_3)
         forward_step(head, 3, 2)
+        when(earlier, scatter_4, head - 1)
         forward_step(head, None, 3)
         save_out(head).start()
-        when(head < KV_HEADS - 2, gather_0, head + 2)
+        when(first, gather_1, 2)
         backward_visits(head, (0, 1))
         scatter_1(head)
-        when(earlier, scatter_5, head - 1)
+        when(first, gather_3, 1)
+        when(second, gather_2, 3)
         backward_visits(head, (2, 3, 4, 5))
         scatter_2(head)
-        when(head < KV_HEADS - 2, gather_1, head + 2)
+        when(first, gather_0, 3)
+        when(earlier, scatter_5, head - 1)
         backward_visits(head, (6, 7, 8))
+        cross_start(head, half_me)
         scatter_3(head)
+        when(first, gather_2, 2)
         close_head(head)
         save_dquery(head).start()
-        when(earlier, scatter_6, head - 1)
+        when(head < KV_HEADS - 1, prepare, head + 1)
         return carry
 
     lax.fori_loop(0, KV_HEADS, head_step, 0)
     scatter_4(KV_HEADS - 1)
+    scatter_6(KV_HEADS - 2)
     scatter_5(KV_HEADS - 1)
     scatter_6(KV_HEADS - 1)
 
@@ -775,8 +794,8 @@
             pltpu.VMEM((ROWS_DEV, HEADS * HEAD_DIM), BF16),
             pltpu.VMEM((ROWS_DEV, HEADS * HEAD_DIM), BF16),
             pltpu.VMEM((KV_HEADS, 4, 2, PAIR, 2 * HEAD_DIM), BF16),
-            pltpu.VMEM((KV_HEADS, 2 * HEAD_DIM, PAIR), BF16),
-            pltpu.VMEM((KV_HEADS, 2 * HEAD_DIM, PAIR), BF16),
+            pltpu.VMEM((KV_HEADS, 2, 2 * HEAD_DIM, HALF), BF16),
+            pltpu.VMEM((KV_HEADS, 2, 2 * HEAD_DIM, HALF), BF16),
             pltpu.VMEM((KV_HEADS, 2, 2 * HEAD_DIM, PAIR), BF16),
             pltpu.VMEM((KV_HEADS, 2, 2 * HEAD_DIM, PAIR), BF16),
             pltpu.VMEM((KV_HEADS, 2 * HEAD_DIM, HALF), BF16),
@@ -791,7 +810,7 @@
             pltpu.VMEM((3, HALF, PAIR), F32),
             pltpu.VMEM((2, VISITS, 2, HALF, PAIR), F32),
             pltpu.VMEM((VISITS, TILES, PAIR, PAIR), BF16),
-            pltpu.VMEM((2, 4, 2, 2 * HEAD_DIM, PAIR), F32),
+            pltpu.VMEM((3, 4, 2, 2 * HEAD_DIM, PAIR), F32),
             pltpu.VMEM((2, 2, 2, HALF, HALF), F32),
             pltpu.VMEM((2, 2, HALF, PAIR), F32),
             pltpu.VMEM(all_rows, F32),
@@ -815,8 +834,8 @@
             pltpu.SemaphoreType.DMA((KV_HEADS, 4)),
             pltpu.SemaphoreType.DMA((KV_HEADS, 4)),
             pltpu.SemaphoreType.DMA((KV_HEADS, 4)),
-            pltpu.SemaphoreType.DMA((KV_HEADS,)),
-            pltpu.SemaphoreType.DMA((KV_HEADS,)),
+            pltpu.SemaphoreType.DMA((KV_HEADS, 2)),
+            pltpu.SemaphoreType.DMA((KV_HEADS, 2)),
             pltpu.SemaphoreType.DMA((KV_HEADS, 2)),
             pltpu.SemaphoreType.DMA((KV_HEADS, 2)),
             pltpu.SemaphoreType.DMA((KV_HEADS,)),

time: 98.2 us -> 94.8 us (0.965)
  the two profiles are of different devices: /device:TPU:20 before, /device:TPU:0 now
where the time goes in v3:
time: 94.8 us; the launch traced here: 94.6 us
  Pallas kernels  94 us (99%)
    pallas_call x1, Pallas kernels, on_device(): pl.pallas_call(functools.partial(kernel, n_dp, n_blocks), out_shape=(wide...  89.8 us
    pallas_call x1, Pallas kernels, carry_out(): pl.pallas_call(functools.partial(carry_kernel, count), out_shape=tuple((j...  4.18 us

profile of v3, /device:TPU:0, one launch (start us, length us, event | category | flops | bytes accessed | tf_op | source)
XLA Modules:
  0.0 94.6 jit_solution(835842426614562264)
XLA Ops:
  0.6 89.8 %shard_map.102 = (bf16[256,4096]{1,0:T(8,128)(2,1)}, bf16[256,4096]{1,0:T(8,128)(2,1)}, bf16[256,512]{1,0:T(8,128)(2,1)}, bf16[256,512]{1,0:T(8,128)(2,1)}) custom-call(bf16[256,4096]{1,0:T(8,128)(2,1)} %q_hbm.1, bf16[256,512]{1,0:T(8,128)(2,1)} %k_ref.1, bf16[256,512]{1,0:T(8,128)(2,1)} %v_ref.1, bf16[256,4096]{1,0:T(8,128)(2,1)} %g_hbm.1, ...), custom_call_target="tpu_custom_call" | custom-call | tf_op jit(solution)/shard_map/pallas_call | solution.py:786
  90.4 4.2 %shard_map.103 = (bf16[256,4096]{1,0:T(8,128)(2,1)}, bf16[256,4096]{1,0:T(8,128)(2,1)}, bf16[256,512]{1,0:T(8,128)(2,1)}, bf16[256,512]{1,0:T(8,128)(2,1)}) custom-call(bf16[256,4096]{1,0:T(8,128)(2,1)} %get-tuple-element.8.refs_0_, bf16[256,4096]{1,0:T(8,128)(2,1)} %get-tuple-element.9.refs_1_, bf16[256,512]{1,0:T(8,128)(2,1)} %get-tuple-element.10.refs_2_, ...), custom_call_target="tpu_custom_call" | custom-call | tf_op jit(solution)/shard_map/pallas_call | solution.py:768

commit v4 on v3

--- a/solution.py
+++ b/solution.py
@@ -690,17 +690,16 @@
         forward_step(head, 1, 0)
         when(first, gather_0, 2)
         when(second, gather_3, 2)
-        when(first, weights_2)
         forward_step(head, 2, 1)
         when(first, gather_2, 1)
         when(second, gather_1, 3)
         when(head > 1, scatter_6, head - 2)
-        when(first, weights_3)
         forward_step(head, 3, 2)
         when(earlier, scatter_4, head - 1)
         forward_step(head, None, 3)
         save_out(head).start()
         when(first, gather_1, 2)
+        when(first, weights_2)
         backward_visits(head, (0, 1))
         scatter_1(head)
         when(first, gather_3, 1)
@@ -713,6 +712,7 @@
         cross_start(head, half_me)
         scatter_3(head)
         when(first, gather_2, 2)
+        when(first, weights_3)
         close_head(head)
         save_dquery(head).start()
         when(head < KV_HEADS - 1, prepare, head + 1)
@@ -734,7 +734,7 @@
     lax.fori_loop(0, KV_HEADS, finish, 0)
 
 
-CHUNKS = 4
+CHUNKS = 2
 
 
 def carry_kernel(count, *refs):

time: 94.8 us -> 89.6 us (0.945)
  Pallas kernels: 94 us -> 88.8 us
    pallas_call x1, Pallas kernels: 89.8 us -> 85.2 us  [on_device(): pl.pallas_call(functools.partial(kernel, n_dp, n_blocks), out_shape=(wide...]
where the time goes in v4:
time: 89.6 us; the launch traced here: 89.5 us
  Pallas kernels  88.8 us (99%)
    pallas_call x1, Pallas kernels, on_device(): pl.pallas_call(functools.partial(kernel, n_dp, n_blocks), out_shape=(wide...  85.2 us
    pallas_call x1, Pallas kernels, carry_out(): pl.pallas_call(functools.partial(carry_kernel, count), out_shape=tuple((j...  3.67 us

profile of v4, /device:TPU:0, one launch (start us, length us, event | category | flops | bytes accessed | tf_op | source)
XLA Modules:
  0.0 89.5 jit_solution(17918088330426640898)
XLA Ops:
  0.6 85.2 %shard_map.102 = (bf16[256,4096]{1,0:T(8,128)(2,1)}, bf16[256,4096]{1,0:T(8,128)(2,1)}, bf16[256,512]{1,0:T(8,128)(2,1)}, bf16[256,512]{1,0:T(8,128)(2,1)}) custom-call(bf16[256,4096]{1,0:T(8,128)(2,1)} %q_hbm.1, bf16[256,512]{1,0:T(8,128)(2,1)} %k_ref.1, bf16[256,512]{1,0:T(8,128)(2,1)} %v_ref.1, bf16[256,4096]{1,0:T(8,128)(2,1)} %g_hbm.1, ...), custom_call_target="tpu_custom_call" | custom-call | tf_op jit(solution)/shard_map/pallas_call | solution.py:786
  85.8 3.7 %shard_map.103 = (bf16[256,4096]{1,0:T(8,128)(2,1)}, bf16[256,4096]{1,0:T(8,128)(2,1)}, bf16[256,512]{1,0:T(8,128)(2,1)}, bf16[256,512]{1,0:T(8,128)(2,1)}) custom-call(bf16[256,4096]{1,0:T(8,128)(2,1)} %get-tuple-element.8.refs_0_, bf16[256,4096]{1,0:T(8,128)(2,1)} %get-tuple-element.9.refs_1_, bf16[256,512]{1,0:T(8,128)(2,1)} %get-tuple-element.10.refs_2_, ...), custom_call_target="tpu_custom_call" | custom-call | tf_op jit(solution)/shard_map/pallas_call | solution.py:768
